TPU v7x, 256 devices: a whole 4x4x8 slice. The times are simulated.
256 devices in a mesh: lat: 32 (over x, z), member: 8 (over y, core).
Axes of the slice: x: 4, y: 4, z: 8, core: 2. Of those that a mesh axis runs over, the one named last changes fastest.
Arguments:
- frames: bfloat16 [8, 256, 512, 128], P('member', 'lat'), may hold values from -6 to 6
- window: int32 [8], replicated, may hold values from 0 to 7, as said below
- targets: bfloat16 [8, 256, 512, 128], P('member', 'lat'), may hold values from -1.5 to 1.5
- w_in: bfloat16 [8, 128, 256], P('member'), may hold values from -0.5 to 0.5
- w_out: bfloat16 [8, 256, 128], P('member'), may hold values from -0.375 to 0.375
- legendre: bfloat16 [256, 256, 256], P('lat'), as said below
- damping: float32 [256], replicated, may hold values from 0.2 to 0.6
Outputs:
- grad_in: float32 [8, 128, 256], P('member')
- grad_out: float32 [8, 256, 128], P('member')
Inputs may be any that keep to these rules, and one draw needn't show every extreme that they name: window[k] // 1 differs for every member k. legendre[m, a, l] is zero for l < m.
All inputs are finite; a program needn't handle non-finite values.
Results may differ from a plain program's by a relative error of at most 0.0011.
Values may be sent and summed in bfloat16 or wider, within the bound.
No kernel may reach another device: no remote copies, remote signals or barrier semaphores. Data moves between devices by JAX's collectives and lax.ppermute only.
A program may use at most 128 MiB of HBM per device.

v0:
```python
import functools
import math

import jax
import jax.numpy as jnp
import numpy as np
from jax import lax
from jax.experimental import pallas as pl
from jax.experimental.pallas import tpu as pltpu
from jax.sharding import Mesh, PartitionSpec as P

LAT = 256
STEPS = 3

EVERY = ("x", "z", "y", "core")
PLANE = ("x", "y", "core")
MEMBER = ("y", "core")

PAIR = 2
SHARE = 4
VMEM = 24 * 1024 * 1024
MOST = 58 * 1024 * 1024


def fourier_matrix(longitudes, orders):
    points = np.arange(longitudes, dtype=np.int32)[:, None]
    angles = (2.0 * math.pi / longitudes * (points * orders[None, :] % longitudes)).astype(
        np.float32
    )
    factor = math.sqrt(2.0 / longitudes)
    paired = np.stack([factor * np.cos(angles), -factor * np.sin(angles)], axis=2)
    return paired.astype(np.float32).reshape(longitudes, 2 * orders.shape[0])


def across(left, right):
    return lax.dot_general(
        left, right, (((0,), (0,)), ((), ())), preferred_element_type=jnp.float32
    )


def exchange(values, axes):
    return lax.all_to_all(values, axes, split_axis=0, concat_axis=0, tiled=True)


def dot(left, right):
    return jnp.dot(left, right, preferred_element_type=jnp.float32)


def row_of(wide, row, rows):
    return wide[pl.ds(row, wide.shape[0] // rows, stride=rows), :]


def side_by_side(parts):
    return jnp.concatenate(parts, axis=1)


def to_grid(wide, fourier, first, rows):
    lines = [row_of(wide, first + i, rows).astype(jnp.bfloat16) for i in range(PAIR)]
    grid = dot(fourier[...], side_by_side(lines))
    return [grid[:, i * 128 : (i + 1) * 128] for i in range(PAIR)]


def to_modes(wide, turned, fields, first, rows):
    spectra = dot(turned[...], side_by_side(fields))
    for i in range(PAIR):
        wide[pl.ds(first + i, spectra.shape[0], stride=rows), :] = spectra[
            :, i * 128 : (i + 1) * 128
        ]


def network(current, w_in, w_out, low_ref, hidden_ref, moved_ref, row):
    low = current.astype(jnp.bfloat16)
    hidden = jnp.tanh(dot(low, w_in[...])).astype(jnp.bfloat16)
    moved = current + dot(hidden, w_out[...])
    low_ref[row] = low
    hidden_ref[row] = hidden
    moved_ref[row] = moved
    return moved.astype(jnp.bfloat16)


def by_pairs(rows):
    def wrapped(run):
        for first in range(0, rows, PAIR):
            run(first)

    return wrapped


def start_kernel(rows, frame, turned, w_in, w_out, spectra, moved, low, hidden, wide):
    @by_pairs(rows)
    def _(first):
        fields = [
            network(frame[row].astype(jnp.float32), w_in, w_out, low, hidden, moved, row)
            for row in range(first, first + PAIR)
        ]
        to_modes(wide, turned, fields, first, rows)

    spectra[...] = wide[...].astype(jnp.bfloat16)


def ahead_kernel(rows, last, returned, before, fourier, turned, w_in, w_out, *rest):
    if last:
        aim, spectra, moved, low, hidden, back, wide = rest
    else:
        spectra, moved, low, hidden, back, wide = rest
    back[...] = returned[...].astype(jnp.float32)

    @by_pairs(rows)
    def _(first):
        grid = to_grid(back, fourier, first, rows)
        fields = [
            network(before[first + i] - grid[i], w_in, w_out, low, hidden, moved, first + i)
            for i in range(PAIR)
        ]
        to_modes(wide, turned, fields, first, rows)

    if last:
        owners = spectra.shape[0]
        spectra[:, 0] = wide[...].astype(jnp.bfloat16).reshape(owners, -1, 128)
        spectra[:, 1] = aim[...].reshape(owners, -1, 128)
    else:
        spectra[...] = wide[...].astype(jnp.bfloat16)


def aim_kernel(rows, target, turned, spectra, wide):
    @by_pairs(rows)
    def _(first):
        to_modes(wide, turned, [target[first + i] for i in range(PAIR)], first, rows)

    spectra[...] = wide[...].astype(jnp.bfloat16)


def adjoint_kernel(rows, first_one, last, returned, base, *rest):
    rest = list(rest)
    target = rest.pop(0) if first_one else None
    low, hidden, fourier, out_t = rest[:4]
    rest = rest[4:]
    if last:
        sum_in, sum_out, sums, back, total_in, total_out = rest
    else:
        turned, in_t = rest[:2]
        rest = rest[2:]
        if first_one:
            sum_in = sum_out = None
        else:
            sum_in, sum_out = rest[:2]
            rest = rest[2:]
        spectra, adjoint, total_in, total_out, back, wide = rest
    back[...] = returned[...].astype(jnp.float32)
    if first_one:
        total_in[...] = jnp.zeros_like(total_in)
        total_out[...] = jnp.zeros_like(total_out)
    else:
        total_in[...] = sum_in[...]
        total_out[...] = sum_out[...]

    @by_pairs(rows)
    def _(first):
        grid = to_grid(back, fourier, first, rows)
        fields = []
        for i in range(PAIR):
            row = first + i
            if first_one:
                pulled = (base[row] - target[row].astype(jnp.float32) - grid[i]) * (1.0 / LAT)
            else:
                pulled = base[row] - grid[i]
            pulled_low = pulled.astype(jnp.bfloat16)
            units = hidden[row]
            total_out[...] += across(pulled_low, units)
            wide_units = units.astype(jnp.float32)
            inner = (dot(pulled_low, out_t[...]) * (1.0 - wide_units * wide_units)).astype(
                jnp.bfloat16
            )
            total_in[...] += across(low[row], inner)
            if not last:
                value = pulled + dot(inner, in_t[...])
                adjoint[row] = value
                fields.append(value.astype(jnp.bfloat16))
        if not last:
            to_modes(wide, turned, fields, first, rows)

    if last:
        height = total_in.shape[0]
        halves = total_in.shape[1] // 128
        for h in range(halves):
            part = slice(h * 128, (h + 1) * 128)
            sums[h * height : (h + 1) * height] = total_in[:, part]
            sums[(halves + h) * height : (halves + h + 1) * height] = total_out[:, part].T
    else:
        spectra[...] = wide[...].astype(jnp.bfloat16)


def parted_kernel(total, grad_in, grad_out):
    height = grad_in.shape[1]
    halves = grad_in.shape[2] // 128
    for h in range(halves):
        grad_in[0, :, h * 128 : (h + 1) * 128] = total[h * height : (h + 1) * height]
    grad_out[0] = total[halves * height :]


def gather_lines(block, k):
    values = block[:, k].astype(jnp.float32)
    owners, pair, channels = values.shape
    values = values.reshape(owners, 2, pair // 2, channels)
    return side_by_side([values[:, r].reshape(-1, channels) for r in range(2)])


def scatter_lines(out, k, values):
    owners = out.shape[0]
    halves = [values[:, r * 128 : (r + 1) * 128].reshape(owners, 1, -1, 128) for r in range(2)]
    lines = jnp.concatenate(halves, axis=1)
    out[:, k] = lines.reshape(owners, -1, 128).astype(jnp.bfloat16)


def filtered(spectra, table, turned, damping):
    coefficients = (dot(turned, spectra) * damping[...]).astype(jnp.bfloat16)
    return dot(table, coefficients)


def filter_kernel(received, table, turned, damping, out):
    @pl.loop(0, table.shape[0], step=SHARE)
    def _(first):
        for k in [first + i for i in range(SHARE)]:
            spectra = gather_lines(received, k).astype(jnp.bfloat16)
            scatter_lines(out, k, filtered(spectra, table[k], turned[k], damping))


def filter_twice_kernel(received, norms, table, turned, damping, out):
    @pl.loop(0, table.shape[0], step=SHARE)
    def _(start):
        for k in [start + i for i in range(SHARE)]:
            spectra = gather_lines(received.at[:, 0], k)
            first = filtered(spectra.astype(jnp.bfloat16), table[k], turned[k], damping)
            second = 2.0 * spectra - gather_lines(received.at[:, 1], k) - norms[k] * first
            scatter_lines(
                out, k, filtered(second.astype(jnp.bfloat16), table[k], turned[k], damping)
            )


def params(limit=VMEM):
    return pltpu.CompilerParams(vmem_limit_bytes=limit)


def shaped(shape, dtype):
    return jax.ShapeDtypeStruct(shape, dtype)


def in_smem():
    return pl.BlockSpec(memory_space=pltpu.SMEM)


def anywhere():
    return pl.BlockSpec(memory_space=pl.ANY)


def in_vmem():
    return pl.BlockSpec(memory_space=pltpu.VMEM)


def paired_kernel(first, second, out, slots, in_sems, out_sems):
    places = [(p, s) for p in range(2) for s in range(first.shape[0])]
    ins, outs = [], []
    for p, s in places:
        source = (first, second)[p].at[s]
        ins.append(pltpu.make_async_copy(source, slots.at[s, p], in_sems.at[p, s]))
        outs.append(pltpu.make_async_copy(slots.at[s, p], out.at[s, p], out_sems.at[p, s]))
    for copy in ins:
        copy.start()
    for copy, after in zip(ins, outs):
        copy.wait()
        after.start()
    for copy in outs:
        copy.wait()


def paired(first, second):
    rows = first.shape[0]
    shape = (rows, 2) + first.shape[1:]
    return pl.pallas_call(
        paired_kernel,
        in_specs=[anywhere()] * 2,
        out_specs=anywhere(),
        out_shape=shaped(shape, first.dtype),
        scratch_shapes=[
            pltpu.VMEM(shape, first.dtype),
            pltpu.SemaphoreType.DMA((2, rows)),
            pltpu.SemaphoreType.DMA((2, rows)),
        ],
        compiler_params=params(MOST),
        name="paired",
    )(first, second)


def chosen_kernel(window, both, frame, held):
    for k in range(frame.shape[0]):
        frame[k] = both[window[k], 0]
        held[k] = both[k, 1]


def chosen(window, both):
    members = both.shape[0]
    out = shaped((members,) + both.shape[2:], both.dtype)
    return pl.pallas_call(
        chosen_kernel,
        in_specs=[in_smem(), in_vmem()],
        out_specs=[in_vmem()] * 2,
        out_shape=[out, out],
        compiler_params=params(),
        name="chosen",
    )(jnp.clip(window, 0, members - 1), both)


def body(frames, window, targets, w_in, w_out, legendre, damping):
    rows, longitudes, channels = frames.shape[1:]
    units = w_in.shape[2]
    size_x, size_z = lax.axis_size("x"), lax.axis_size("z")
    members = lax.axis_size(MEMBER)
    owners = size_x * members
    modes = legendre.shape[0]
    degrees = legendre.shape[2]
    lines = owners * 2 * modes * rows
    width = 2 * modes * owners
    place = lax.axis_index(MEMBER)
    plane = lax.axis_index("z")
    bf16, f32 = jnp.bfloat16, jnp.float32

    swap = [
        ((x * size_z + z) * members + k, (x * size_z + k) * members + z)
        for x in range(size_x)
        for z in range(size_z)
        for k in range(members)
    ]
    first_layer = lax.ppermute(w_in[0], EVERY, swap)
    second_layer = lax.ppermute(w_out[0], EVERY, swap)

    table = lax.dynamic_index_in_dim(legendre, place, 0, keepdims=False)
    table = table.reshape(size_x, size_z, rows, degrees)
    table = table.transpose(0, 2, 1, 3).reshape(owners * rows, degrees)
    table, window = lax.optimization_barrier((table, window))
    table = lax.all_gather(table, "z")

    both = exchange(paired(frames[0], targets[0]), MEMBER)
    both, table, first_layer, second_layer = lax.optimization_barrier(
        (both, table, first_layer, second_layer)
    )
    frame, held = chosen(window, both)
    frame = exchange(frame, "z")
    held, frame = lax.optimization_barrier((held, frame))
    held = lax.all_gather(held, "z")

    table = table.reshape(modes, owners * rows, degrees)
    turned_table = table.transpose(0, 2, 1)

    ordered = np.arange(modes * owners, dtype=np.int32)
    ordered = ordered.reshape(size_x, size_z, members).transpose(0, 2, 1).reshape(-1)
    matrix = fourier_matrix(longitudes, ordered)
    fourier = jnp.asarray(matrix).astype(bf16)
    turned = jnp.asarray(np.ascontiguousarray(matrix.T)).astype(bf16)

    mode = (lax.axis_index("x") * size_z + jnp.arange(modes)) * members + place
    norms = jnp.where(mode[:, None] == 0, jnp.array([[2.0, 0.0]]), 1.0)
    norms = jnp.repeat(norms, channels, axis=1).reshape(modes, 1, 2 * channels)
    decay = jnp.broadcast_to(damping[:, None], (degrees, 2 * channels))

    shape = (rows, longitudes, channels)
    deep_shape = (rows, longitudes, units)
    buffer = pltpu.VMEM((lines, channels), f32)

    def forward(returned, before, aim=None):
        last = aim is not None
        if returned is None:
            kernel = functools.partial(start_kernel, rows)
            operands = [before, turned, first_layer, second_layer]
            scratch = [buffer]
        else:
            kernel = functools.partial(ahead_kernel, rows, last)
            operands = [returned, before, fourier, turned, first_layer, second_layer]
            operands += [aim] if last else []
            scratch = [buffer, buffer]
        cells = rows * longitudes
        return pl.pallas_call(
            kernel,
            out_shape=[
                shaped((owners, 2, lines // owners, channels) if last else (lines, channels), bf16),
                shaped(shape, f32),
                shaped(shape, bf16),
                shaped(deep_shape, bf16),
            ],
            scratch_shapes=scratch,
            compiler_params=params(),
            cost_estimate=pl.CostEstimate(
                flops=4 * cells * channels * (units + width),
                bytes_accessed=9 * cells * channels * 2,
                transcendentals=cells * units,
            ),
            name="forward",
        )(*operands)

    def transformed(target):
        return pl.pallas_call(
            functools.partial(aim_kernel, rows),
            out_shape=shaped((lines, channels), bf16),
            scratch_shapes=[buffer],
            compiler_params=params(),
            cost_estimate=pl.CostEstimate(
                flops=2 * rows * longitudes * channels * width,
                bytes_accessed=4 * lines * channels,
                transcendentals=0,
            ),
            name="aim",
        )(target, turned)

    def adjoint_of(returned, base, low, hidden, sums, target=None, last=False):
        first_one = target is not None
        operands = [returned, base] + ([target] if first_one else [])
        operands += [low, hidden, fourier, out_t]
        sum_shape = shaped(first_layer.shape, f32)
        accumulators = [pltpu.VMEM(first_layer.shape, f32)] * 2
        if last:
            operands += list(sums)
            outs = shaped((2 * units, channels), f32)
            scratch = [buffer] + accumulators
        else:
            operands += [turned, in_t] + ([] if first_one else list(sums))
            outs = [shaped((lines, channels), bf16), shaped(shape, f32), sum_shape, sum_shape]
            scratch = [buffer, buffer]
        cells = rows * longitudes
        return pl.pallas_call(
            functools.partial(adjoint_kernel, rows, first_one, last),
            out_shape=outs,
            scratch_shapes=scratch,
            compiler_params=params(),
            cost_estimate=pl.CostEstimate(
                flops=4 * cells * channels * (2 * units + width),
                bytes_accessed=11 * cells * channels * 2,
                transcendentals=0,
            ),
            name="adjoint",
        )(*operands)

    blocks = (owners, modes, 2 * rows, channels)

    def filtering(received):
        out = pl.pallas_call(
            filter_kernel,
            out_shape=shaped(blocks, bf16),
            compiler_params=params(),
            cost_estimate=pl.CostEstimate(
                flops=8 * lines * channels * degrees,
                bytes_accessed=8 * lines * channels,
                transcendentals=0,
            ),
            name="filter",
        )(received.reshape(blocks), table, turned_table, decay)
        return out.reshape(lines, channels)

    def filtering_twice(received):
        received = received.reshape(owners, 2, modes, 2 * rows, channels)
        out = pl.pallas_call(
            filter_twice_kernel,
            out_shape=shaped(blocks, bf16),
            compiler_params=params(),
            cost_estimate=pl.CostEstimate(
                flops=16 * lines * channels * degrees,
                bytes_accessed=10 * lines * channels,
                transcendentals=0,
            ),
            name="filter_twice",
        )(received, norms, table, turned_table, decay)
        return out.reshape(lines, channels)

    in_t, out_t = first_layer.T, second_layer.T
    table, turned_table, decay, norms, in_t, out_t, first_layer, second_layer, frame = (
        lax.optimization_barrier(
            (table, turned_table, decay, norms, in_t, out_t, first_layer, second_layer, frame)
        )
    )
    history = []
    moved, returned, aim = frame, None, None
    for step in range(STEPS):
        if step == STEPS - 1:
            held, returned = lax.optimization_barrier((held, returned))
            target = lax.dynamic_index_in_dim(held, plane, 1, keepdims=False)
            aim = transformed(target)
        spectra, moved, low, hidden = forward(returned, moved, aim)
        history.append((low, hidden))
        if step < STEPS - 1:
            returned = exchange(filtering(exchange(spectra, PLANE)), PLANE)
    received = exchange(spectra, PLANE)
    returned = exchange(filtering_twice(received), PLANE)

    sums = None
    adjoint = moved
    for step in reversed(range(1, STEPS)):
        low, hidden = history[step]
        spectra, adjoint, *sums = adjoint_of(
            returned, adjoint, low, hidden, sums, target if step == STEPS - 1 else None
        )
        returned = exchange(filtering(exchange(spectra, PLANE)), PLANE)
    low, hidden = history[0]
    sums = adjoint_of(returned, adjoint, low, hidden, sums, None, True)

    height = sums.shape[0] // owners
    pieces = exchange(sums, PLANE).reshape(owners, height, 128).sum(axis=0)
    around = exchange(jnp.broadcast_to(pieces[None], (size_z, height, 128)), "z")
    spread = jnp.broadcast_to(around[None], (size_x, members, height, 128))
    total = exchange(spread.reshape(-1, 128), PLANE)
    return tuple(
        pl.pallas_call(
            parted_kernel,
            out_shape=[shaped(w_in.shape, f32), shaped(w_out.shape, f32)],
            compiler_params=params(),
            name="parted",
        )(total)
    )


def solution(mesh):
    fine = Mesh(mesh.devices.reshape(4, 8, 4, 2), EVERY)
    lat, member = ("x", "z"), MEMBER
    return jax.shard_map(
        body,
        mesh=fine,
        in_specs=(
            P(member, lat, None, None),
            P(),
            P(member, lat, None, None),
            P(member, None, None),
            P(member, None, None),
            P(lat, None, None),
            P(),
        ),
        out_specs=(P(member, None, None), P(member, None, None)),
        check_vma=False,
    )
```

profile of v0, /device:TPU:1, one launch (start us, length us, event | category | flops | bytes accessed | tf_op | source)
XLA Modules:
  0.0 392.4 jit_solution(8209665628015391179)
XLA Ops:
  11.8 6.9 %all-to-all-start = ((bf16[8,2,512,128]{3,2,1,0:T(8,128)(2,1)}), bf16[8,2,512,128]{3,2,1,0:T(8,128)(2,1)S(1)}, u32[]{:S(2)}, u32[]{:S(2)}) async-start(bf16[8,2,512,128]{3,2,1,0:T(8,128)(2,1)} %paired.1), calls=%async_computation | async-start | bytes 4194304 | tf_op jit(solution)/shard_map/all_to_all | solution.py:42
  21.7 2.9 collective-permute-start.1
  24.7 5.5 %collective-permute-done.1 = bf16[256,128]{0,1:T(8,128)(2,1)S(1)} collective-permute-done((bf16[256,128]{0,1:T(8,128)(2,1)S(1)}, bf16[256,128]{0,1:T(8,128)(2,1)S(1)}, u32[]{:S(2)}, u32[]{:S(2)}) %collective-permute-start.1) | collective-permute-done | bytes 65568 | tf_op jit(solution)/shard_map/ppermute | solution.py:334
  30.2 22.2 %all-gather.5.cloned.1.call-done = bf16[2048,256]{1,0:T(8,128)(2,1)} async-done(((bf16[256,256]{1,0:T(8,128)(2,1)}), bf16[2048,256]{1,0:T(8,128)(2,1)}) %all-gather.5.cloned.1.call-update) | async-done | bytes 1048592 | tf_op jit(solution)/shard_map/all_gather | solution.py:340
  54.1 31.1 %all_to_all.132.frame = bf16[8,512,128]{2,1,0:T(8,128)(2,1)} all-to-all(bf16[8,512,128]{2,1,0:T(8,128)(2,1)S(1)} %get-tuple-element.47), channel_id=1, replica_groups=mesh['x'=4,'z'=8,'y'=4,'core'=2] {'z'}, dimensions={0} | all-to-all | bytes 2097152 | tf_op jit(solution)/shard_map/all_to_all | solution.py:42
  90.3 27.3 %all_to_all.133 = bf16[32,128,128]{2,1,0:T(8,128)(2,1)S(1)} all-to-all(bf16[32,128,128]{2,1,0:T(8,128)(2,1)S(1)} %bitcast.64), channel_id=1, replica_groups=mesh['x'=4,'z'=8,'y'=4,'core'=2] {'x','y','core'}, dimensions={0} | all-to-all | bytes 2097152 | tf_op jit(solution)/shard_map/all_to_all | solution.py:42
  118.9 20.8 %all_to_all.134 = bf16[32,128,128]{2,1,0:T(8,128)(2,1)S(1)} all-to-all(bf16[32,128,128]{2,1,0:T(8,128)(2,1)S(1)} %bitcast.52), channel_id=1, replica_groups=mesh['x'=4,'z'=8,'y'=4,'core'=2] {'x','y','core'}, dimensions={0} | all-to-all | bytes 2097152 | tf_op jit(solution)/shard_map/all_to_all | solution.py:42
  139.7 3.6 forward.4
  143.3 20.7 %all_to_all.135 = bf16[32,128,128]{2,1,0:T(8,128)(2,1)S(1)} all-to-all(bf16[32,128,128]{2,1,0:T(8,128)(2,1)S(1)} %bitcast.63), channel_id=1, replica_groups=mesh['x'=4,'z'=8,'y'=4,'core'=2] {'x','y','core'}, dimensions={0} | all-to-all | bytes 2097152 | tf_op jit(solution)/shard_map/all_to_all | solution.py:42
  166.2 4.6 %all-to-all-start.5 = ((bf16[32,128,128]{2,1,0:T(8,128)(2,1)}), bf16[32,128,128]{2,1,0:T(8,128)(2,1)}, u32[]{:S(2)}, u32[]{:S(2)}) async-start(bf16[32,128,128]{2,1,0:T(8,128)(2,1)} %bitcast.19), calls=%async_computation.5 | async-start | bytes 2097152 | tf_op jit(solution)/shard_map/all_to_all | solution.py:42
  170.8 16.8 %all-to-all-done.5 = bf16[32,128,128]{2,1,0:T(8,128)(2,1)} async-done(((bf16[32,128,128]{2,1,0:T(8,128)(2,1)}), bf16[32,128,128]{2,1,0:T(8,128)(2,1)}, u32[]{:S(2)}, u32[]{:S(2)}) %all-to-all-start.5) | async-done | bytes 1048608 | tf_op jit(solution)/shard_map/all_to_all | solution.py:42
  190.0 4.8 %forward.5 = (bf16[32,2,128,128]{3,2,1,0:T(8,128)(2,1)S(1)}, f32[8,512,128]{2,1,0:T(8,128)S(1)}, bf16[8,512,128]{2,1,0:T(8,128)(2,1)S(1)}, bf16[8,512,256]{2,1,0:T(8,128)(2,1)S(1)}) custom-call(bf16[4096,128]{1,0:T(8,128)(2,1)} %bitcast.20.returned, f32[8,512,128]{2,1,0:T(8,128)S(1)} %copy-done.20, bf16[512,512]{1,0:T(8,128)(2,1)S(1)} %copy-done.6, ...), custom_call_target="tpu_custom_call" | custom-call | flops 1610612736 | bytes 9437184 | tf_op jit(solution)/shard_map/forward/pallas_call | solution.py:381
  194.8 31.9 %all_to_all.136 = bf16[32,2,128,128]{3,2,1,0:T(8,128)(2,1)S(1)} all-to-all(bf16[32,2,128,128]{3,2,1,0:T(8,128)(2,1)S(1)} %get-tuple-element.65), channel_id=1, replica_groups=mesh['x'=4,'z'=8,'y'=4,'core'=2] {'x','y','core'}, dimensions={0} | all-to-all | bytes 4194304 | tf_op jit(solution)/shard_map/all_to_all | solution.py:42
  226.7 4.2 %filter_twice.1 = bf16[32,8,16,128]{3,2,1,0:T(8,128)(2,1)S(1)} custom-call(bf16[32,2,8,16,128]{4,3,2,1,0:T(8,128)(2,1)S(1)} %bitcast.57, f32[8,1,256]{2,1,0:T(1,128)S(1)} %bitcast.73, bf16[8,256,256]{2,1,0:T(8,128)(2,1)S(1)} %bitcast.41, bf16[8,256,256]{2,1,0:T(8,128)(2,1)S(1)} %bitcast.46, f32[256,256]{1,0:T(8,128)S(1)} %broadcast_in_dim.44.damping), custom_call_target="tpu_custom_call" | custom-call | flops 2147483648 | bytes 5242880 | tf_op jit(solution)/shard_map/filter_twice/pallas_call | solution.py:459
  230.9 20.7 %all_to_all.137 = bf16[32,128,128]{2,1,0:T(8,128)(2,1)S(1)} all-to-all(bf16[32,128,128]{2,1,0:T(8,128)(2,1)S(1)} %bitcast.65), channel_id=1, replica_groups=mesh['x'=4,'z'=8,'y'=4,'core'=2] {'x','y','core'}, dimensions={0} | all-to-all | bytes 2097152 | tf_op jit(solution)/shard_map/all_to_all | solution.py:42
  251.6 4.6 %adjoint.3 = (bf16[4096,128]{1,0:T(8,128)(2,1)S(1)}, f32[8,512,128]{2,1,0:T(8,128)S(1)}, f32[128,256]{1,0:T(8,128)S(1)}, f32[128,256]{1,0:T(8,128)S(1)}) custom-call(bf16[4096,128]{1,0:T(8,128)(2,1)S(1)} %bitcast.56, f32[8,512,128]{2,1,0:T(8,128)S(1)} %get-tuple-element.67.base, bf16[8,512,128]{2,1,0:T(8,128)(2,1)S(1)} %dynamic-slice_bitcast_fusion.target.rest_0_, ...), custom_call_target="tpu_custom_call" | custom-call | flops 2147483648 | bytes 11534336 | tf_op jit(solution)/shard_map/adjoint/pallas_call | solution.py:428
  256.1 20.7 %all_to_all.138 = bf16[32,128,128]{2,1,0:T(8,128)(2,1)S(1)} all-to-all(bf16[32,128,128]{2,1,0:T(8,128)(2,1)S(1)} %bitcast.61), channel_id=1, replica_groups=mesh['x'=4,'z'=8,'y'=4,'core'=2] {'x','y','core'}, dimensions={0} | all-to-all | bytes 2097152 | tf_op jit(solution)/shard_map/all_to_all | solution.py:42
  278.0 20.8 %all_to_all.139 = bf16[32,128,128]{2,1,0:T(8,128)(2,1)S(1)} all-to-all(bf16[32,128,128]{2,1,0:T(8,128)(2,1)S(1)} %bitcast.55), channel_id=1, replica_groups=mesh['x'=4,'z'=8,'y'=4,'core'=2] {'x','y','core'}, dimensions={0} | all-to-all | bytes 2097152 | tf_op jit(solution)/shard_map/all_to_all | solution.py:42
  298.8 4.6 %adjoint.4 = (bf16[4096,128]{1,0:T(8,128)(2,1)S(1)}, f32[8,512,128]{2,1,0:T(8,128)S(1)}, f32[128,256]{1,0:T(8,128)S(1)}, f32[128,256]{1,0:T(8,128)S(1)}) custom-call(bf16[4096,128]{1,0:T(8,128)(2,1)S(1)} %bitcast.58, f32[8,512,128]{2,1,0:T(8,128)S(1)} %get-tuple-element.73.base, bf16[8,512,128]{2,1,0:T(8,128)(2,1)S(1)} %copy-done.16, ...), custom_call_target="tpu_custom_call" | custom-call | flops 2147483648 | bytes 11534336 | tf_op jit(solution)/shard_map/adjoint/pallas_call | solution.py:428
  303.4 20.7 %all_to_all.140 = bf16[32,128,128]{2,1,0:T(8,128)(2,1)S(1)} all-to-all(bf16[32,128,128]{2,1,0:T(8,128)(2,1)S(1)} %bitcast.59), channel_id=1, replica_groups=mesh['x'=4,'z'=8,'y'=4,'core'=2] {'x','y','core'}, dimensions={0} | all-to-all | bytes 2097152 | tf_op jit(solution)/shard_map/all_to_all | solution.py:42
  325.3 20.8 %all_to_all.141 = bf16[32,128,128]{2,1,0:T(8,128)(2,1)S(1)} all-to-all(bf16[32,128,128]{2,1,0:T(8,128)(2,1)S(1)} %bitcast.50), channel_id=1, replica_groups=mesh['x'=4,'z'=8,'y'=4,'core'=2] {'x','y','core'}, dimensions={0} | all-to-all | bytes 2097152 | tf_op jit(solution)/shard_map/all_to_all | solution.py:42
  348.8 12.7 %all_to_all.142 = f32[32,16,128]{2,1,0:T(8,128)S(1)} all-to-all(f32[32,16,128]{2,1,0:T(8,128)S(1)} %bitcast.72), channel_id=1, replica_groups=mesh['x'=4,'z'=8,'y'=4,'core'=2] {'x','y','core'}, dimensions={0} | all-to-all | bytes 524288 | tf_op jit(solution)/shard_map/all_to_all | solution.py:42
  361.6 9.5 %all_to_all.143 = f32[8,16,128]{2,1,0:T(8,128)S(1)} all-to-all(f32[8,16,128]{2,1,0:T(8,128)S(1)} %broadcast_in_dim.50), channel_id=1, replica_groups=mesh['x'=4,'z'=8,'y'=4,'core'=2] {'z'}, dimensions={0} | all-to-all | bytes 131072 | tf_op jit(solution)/shard_map/all_to_all | solution.py:42
  371.1 13.7 %all_to_all.144 = f32[32,16,128]{2,1,0:T(8,128)S(1)} all-to-all(f32[32,16,128]{2,1,0:T(8,128)S(1)} %bitcast.74), channel_id=1, replica_groups=mesh['x'=4,'z'=8,'y'=4,'core'=2] {'x','y','core'}, dimensions={0} | all-to-all | bytes 524288 | tf_op jit(solution)/shard_map/all_to_all | solution.py:42
  (90 shorter events, 26.0 us)
Async XLA Ops:
  7.2 45.2 %all-gather.5.cloned.1.call-start = ((), (), s32[]{:S(2)}) async-start(), calls=%async_computation.15 | async-start | bytes 1179648 | tf_op jit(solution)/shard_map/all_gather | solution.py:340
  11.8 6.9 %copy-start.23 = (bf16[1,128,256]{2,1,0:T(8,128)(2,1)S(1)}, bf16[1,128,256]{2,1,0:T(8,128)(2,1)}, u32[]{:S(2)}) copy-start(bf16[1,128,256]{2,1,0:T(8,128)(2,1)} %param.13) | copy-start | bytes 196612
  11.8 9.8 %copy-start.24 = (bf16[1,256,128]{2,1,0:T(8,128)(2,1)S(1)}, bf16[1,256,128]{2,1,0:T(8,128)(2,1)}, u32[]{:S(2)}) copy-start(bf16[1,256,128]{2,1,0:T(8,128)(2,1)} %param.14) | copy-start | bytes 196612
  11.8 12.7 %copy-start.27 = (s32[8]{0:T(128)S(1)}, s32[8]{0:T(128)}, u32[]{:S(2)}) copy-start(s32[8]{0:T(128)} %param.11) | copy-start | bytes 100
  11.8 40.6 %all-to-all-start = ((bf16[8,2,512,128]{3,2,1,0:T(8,128)(2,1)}), bf16[8,2,512,128]{3,2,1,0:T(8,128)(2,1)S(1)}, u32[]{:S(2)}, u32[]{:S(2)}) async-start(bf16[8,2,512,128]{3,2,1,0:T(8,128)(2,1)} %paired.1), calls=%async_computation | async-start | bytes 4194304 | tf_op jit(solution)/shard_map/all_to_all | solution.py:42
  18.7 168.9 %all-gather.7.cloned.1.call-start = ((), (), s32[]{:S(2)}) async-start(), calls=%async_computation.16 | async-start | bytes 9437184 | tf_op jit(solution)/shard_map/all_gather | solution.py:349
  18.8 5.9 %collective-permute-start = (bf16[128,256]{0,1:T(8,128)(2,1)S(1)}, bf16[128,256]{0,1:T(8,128)(2,1)S(1)}, u32[]{:S(2)}, u32[]{:S(2)}) collective-permute-start(bf16[128,256]{0,1:T(8,128)(2,1)S(1)} %bitcast.80), channel_id=1, source_target_pairs={{0,0},{1,8},{2,16},{3,24},{4,32},{5,40},{6,48},{7,56},{8,1},{9,9},... | collective-permute-start | bytes 196616 | tf_op jit(solution)/shard_map/ppermute | solution.py:333
  21.7 8.6 %collective-permute-start.1 = (bf16[256,128]{0,1:T(8,128)(2,1)S(1)}, bf16[256,128]{0,1:T(8,128)(2,1)S(1)}, u32[]{:S(2)}, u32[]{:S(2)}) collective-permute-start(bf16[256,128]{0,1:T(8,128)(2,1)S(1)} %bitcast.81), channel_id=1, source_target_pairs={{0,0},{1,8},{2,16},{3,24},{4,32},{5,40},{6,48},{7,56},{8,1},{9,9},... | collective-permute-start | bytes 196616 | tf_op jit(solution)/shard_map/ppermute | solution.py:334
  53.1 32.2 %copy-start.26 = (f32[2]{0:T(128)S(1)}, f32[2]{0:T(128)}, u32[]{:S(2)}) copy-start(f32[2]{0:T(128)} %constant.52) | copy-start | bytes 28
  53.1 32.3 %copy-start.2 = (bf16[2048,256]{1,0:T(8,128)(2,1)S(1)}, bf16[2048,256]{1,0:T(8,128)(2,1)}, u32[]{:S(2)}) copy-start(bf16[2048,256]{1,0:T(8,128)(2,1)} %all-gather.5.cloned.1.call-done) | copy-start | bytes 3145732
  90.3 28.5 %copy-start.17 = (bf16[8,512,256]{2,1,0:T(8,128)(2,1)}, bf16[8,512,256]{2,1,0:T(8,128)(2,1)S(1)}, u32[]{:S(2)}) copy-start(bf16[8,512,256]{2,1,0:T(8,128)(2,1)S(1)} %get-tuple-element.81.rest_1_) | copy-start | bytes 6291460
  90.3 28.5 %copy-start.21 = (bf16[8,512,128]{2,1,0:T(8,128)(2,1)}, bf16[8,512,128]{2,1,0:T(8,128)(2,1)S(1)}, u32[]{:S(2)}) copy-start(bf16[8,512,128]{2,1,0:T(8,128)(2,1)S(1)} %get-tuple-element.80.rest_0_) | copy-start | bytes 3145732
  118.8 20.8 %copy-start.6 = (bf16[512,512]{1,0:T(8,128)(2,1)S(1)}, bf16[512,512]{1,0:T(8,128)(2,1)}, u32[]{:S(2)}) copy-start(bf16[512,512]{1,0:T(8,128)(2,1)} %constant.54.fourier.rest_3_.rest_2_) | copy-start | bytes 1572868
  118.8 20.8 %copy-start.8 = (bf16[128,256]{1,0:T(8,128)(2,1)S(1)}, bf16[128,256]{1,0:T(8,128)(2,1)}, u32[]{:S(2)}) copy-start(bf16[128,256]{1,0:T(8,128)(2,1)} %copy-done.7) | copy-start | bytes 196612
  118.9 20.8 %copy-start.11 = (bf16[256,128]{1,0:T(8,128)(2,1)S(1)}, bf16[256,128]{1,0:T(8,128)(2,1)}, u32[]{:S(2)}) copy-start(bf16[256,128]{1,0:T(8,128)(2,1)} %copy-done.10) | copy-start | bytes 196612
  143.2 22.9 %copy-start.13 = (bf16[8,512,256]{2,1,0:T(8,128)(2,1)}, bf16[8,512,256]{2,1,0:T(8,128)(2,1)S(1)}, u32[]{:S(2)}) copy-start(bf16[8,512,256]{2,1,0:T(8,128)(2,1)S(1)} %get-tuple-element.75.rest_1_) | copy-start | bytes 6291460
  143.2 22.9 %copy-start.15 = (bf16[8,512,128]{2,1,0:T(8,128)(2,1)}, bf16[8,512,128]{2,1,0:T(8,128)(2,1)S(1)}, u32[]{:S(2)}) copy-start(bf16[8,512,128]{2,1,0:T(8,128)(2,1)S(1)} %get-tuple-element.74.rest_0_) | copy-start | bytes 3145732
  143.3 22.9 %copy-start.19 = (f32[8,512,128]{2,1,0:T(8,128)}, f32[8,512,128]{2,1,0:T(8,128)S(1)}, u32[]{:S(2)}) copy-start(f32[8,512,128]{2,1,0:T(8,128)S(1)} %get-tuple-element.63.before) | copy-start | bytes 6291460
  166.2 21.4 %all-to-all-start.5 = ((bf16[32,128,128]{2,1,0:T(8,128)(2,1)}), bf16[32,128,128]{2,1,0:T(8,128)(2,1)}, u32[]{:S(2)}, u32[]{:S(2)}) async-start(bf16[32,128,128]{2,1,0:T(8,128)(2,1)} %bitcast.19), calls=%async_computation.5 | async-start | bytes 2097152 | tf_op jit(solution)/shard_map/all_to_all | solution.py:42
  276.8 22.0 %copy-start.16 = (bf16[8,512,128]{2,1,0:T(8,128)(2,1)S(1)}, bf16[8,512,128]{2,1,0:T(8,128)(2,1)}, u32[]{:S(2)}) copy-start(bf16[8,512,128]{2,1,0:T(8,128)(2,1)} %copy-done.15) | copy-start | bytes 3145732
  278.0 20.8 %copy-start.14 = (bf16[8,512,256]{2,1,0:T(8,128)(2,1)S(1)}, bf16[8,512,256]{2,1,0:T(8,128)(2,1)}, u32[]{:S(2)}) copy-start(bf16[8,512,256]{2,1,0:T(8,128)(2,1)} %copy-done.13) | copy-start | bytes 6291460
  324.1 22.0 %copy-start.22 = (bf16[8,512,128]{2,1,0:T(8,128)(2,1)S(1)}, bf16[8,512,128]{2,1,0:T(8,128)(2,1)}, u32[]{:S(2)}) copy-start(bf16[8,512,128]{2,1,0:T(8,128)(2,1)} %copy-done.21) | copy-start | bytes 3145732
  325.3 20.8 %copy-start.18 = (bf16[8,512,256]{2,1,0:T(8,128)(2,1)S(1)}, bf16[8,512,256]{2,1,0:T(8,128)(2,1)}, u32[]{:S(2)}) copy-start(bf16[8,512,256]{2,1,0:T(8,128)(2,1)} %copy-done.17) | copy-start | bytes 6291460
  346.1 39.4 %copy-start.1 = (bf16[8,256,256]{2,1,0:T(8,128)(2,1)S(1)}, bf16[8,256,256]{2,1,0:T(8,128)(2,1)}, u32[]{:S(2)}) copy-start(bf16[8,256,256]{2,1,0:T(8,128)(2,1)} %param.15) | copy-start | bytes 3145732
  (10 other events, 19.2 us)
Sparse Core Ops, SparseCore 0:
  10.4 41.9 all-gather.4
  85.4 93.3 all-gather.6
where the time goes:
time: 393 us; the launch traced here: 392 us
  blocking collectives  271 us (69%)
  waiting for transfers between devices  44.7 us (11%)
  Pallas kernels  37.9 us (10%)
  starting transfers between devices  17.1 us (4%)
  between operations  14.5 us (4%)
  local copies, waits for them, and re-layouts  6.78 us (2%)
    all_to_all x13, blocking collectives, exchange(): return lax.all_to_all(values, axes, split_axis=0, concat_axis=0, tiled=True)  271 us
    all_gather x1, waiting for transfers between devices, body(): table = lax.all_gather(table, 'z')  22.2 us
    all_to_all x2, waiting for transfers between devices, exchange(): return lax.all_to_all(values, axes, split_axis=0, concat_axis=0, tiled=True)  16.8 us
    pallas_call x3, Pallas kernels, adjoint_of(): pl.pallas_call(functools.partial(adjoint_kernel, rows, first_one, last),...  11.8 us
    all_to_all x2, starting transfers between devices, exchange(): return lax.all_to_all(values, axes, split_axis=0, concat_axis=0, tiled=True)  11.5 us
    pallas_call x3, Pallas kernels, forward(): pl.pallas_call(kernel, out_shape=[shaped((owners, 2, lines // owners, cha...  11.1 us
  transfers between devices with their start and end apart: 6, of which 4 were waited for; matrix products, arithmetic and copies ran while one was open for 0% of the time, Pallas kernels for 3%

commit v1 on v0

--- a/solution.py
+++ b/solution.py
@@ -17,7 +17,7 @@
 MEMBER = ("y", "core")
 
 PAIR = 2
-SHARE = 4
+SHARE = 8
 VMEM = 24 * 1024 * 1024
 MOST = 58 * 1024 * 1024
 
@@ -257,7 +257,7 @@
     return pl.BlockSpec(memory_space=pltpu.VMEM)
 
 
-def paired_kernel(first, second, out, slots, in_sems, out_sems):
+def paired_kernel(first, second, after, out, slots, in_sems, out_sems):
     places = [(p, s) for p in range(2) for s in range(first.shape[0])]
     ins, outs = [], []
     for p, s in places:
@@ -273,12 +273,12 @@
         copy.wait()
 
 
-def paired(first, second):
+def paired(first, second, after):
     rows = first.shape[0]
     shape = (rows, 2) + first.shape[1:]
     return pl.pallas_call(
         paired_kernel,
-        in_specs=[anywhere()] * 2,
+        in_specs=[anywhere()] * 3,
         out_specs=anywhere(),
         out_shape=shaped(shape, first.dtype),
         scratch_shapes=[
@@ -288,7 +288,7 @@
         ],
         compiler_params=params(MOST),
         name="paired",
-    )(first, second)
+    )(first, second, after)
 
 
 def chosen_kernel(window, both, frame, held):
@@ -336,16 +336,14 @@
     table = lax.dynamic_index_in_dim(legendre, place, 0, keepdims=False)
     table = table.reshape(size_x, size_z, rows, degrees)
     table = table.transpose(0, 2, 1, 3).reshape(owners * rows, degrees)
-    table, window = lax.optimization_barrier((table, window))
+    both = paired(frames[0], targets[0], table)
     table = lax.all_gather(table, "z")
 
-    both = exchange(paired(frames[0], targets[0]), MEMBER)
-    both, table, first_layer, second_layer = lax.optimization_barrier(
-        (both, table, first_layer, second_layer)
-    )
+    both = exchange(both, MEMBER)
+    both, first_layer, second_layer = lax.optimization_barrier((both, first_layer, second_layer))
     frame, held = chosen(window, both)
     frame = exchange(frame, "z")
-    held, frame = lax.optimization_barrier((held, frame))
+    held, frame, table = lax.optimization_barrier((held, frame, table))
     held = lax.all_gather(held, "z")
 
     table = table.reshape(modes, owners * rows, degrees)

time: 393 us -> 392 us (level)
  blocking collectives: 271 us -> 237 us
  waiting for transfers between devices: 44.7 us -> 67.8 us
  starting transfers between devices: 17.1 us -> 28 us
    all_to_all x2 -> x3, waiting for transfers between devices: 16.8 us -> 57.9 us  [exchange(): return lax.all_to_all(values, axes, split_axis=0, concat_axis=0, tiled=True)]
    all_to_all x13 -> x12, blocking collectives: 271 us -> 237 us  [exchange(): return lax.all_to_all(values, axes, split_axis=0, concat_axis=0, tiled=True)]
    all_gather x1, waiting for transfers between devices: 22.2 us -> 5.58 us  [body(): table = lax.all_gather(table, 'z')]
    all_to_all x2 -> x3, starting transfers between devices: 11.5 us -> 22.4 us  [exchange(): return lax.all_to_all(values, axes, split_axis=0, concat_axis=0, tiled=True)]
  transfers between devices with their start and end apart: 6 -> 7, of which waited for: 4 -> 6; matrix products, arithmetic and copies ran while one was open for 0% -> 1% of each run, Pallas kernels for 3% -> 3%
where the time goes in v1:
time: 392 us; the launch traced here: 391 us
  blocking collectives  237 us (60%)
  waiting for transfers between devices  67.8 us (17%)
  Pallas kernels  37.6 us (10%)
  starting transfers between devices  28 us (7%)
  between operations  14.5 us (4%)
  local copies, waits for them, and re-layouts  5.59 us (1%)
    all_to_all x12, blocking collectives, exchange(): return lax.all_to_all(values, axes, split_axis=0, concat_axis=0, tiled=True)  237 us
    all_to_all x3, waiting for transfers between devices, exchange(): return lax.all_to_all(values, axes, split_axis=0, concat_axis=0, tiled=True)  57.9 us
    all_to_all x3, starting transfers between devices, exchange(): return lax.all_to_all(values, axes, split_axis=0, concat_axis=0, tiled=True)  22.4 us
    pallas_call x3, Pallas kernels, adjoint_of(): pl.pallas_call(functools.partial(adjoint_kernel, rows, first_one, last),...  11.8 us
    pallas_call x3, Pallas kernels, forward(): pl.pallas_call(kernel, out_shape=[shaped((owners, 2, lines // owners, cha...  11.1 us
  transfers between devices with their start and end apart: 7, of which 6 were waited for; matrix products, arithmetic and copies ran while one was open for 1% of the time, Pallas kernels for 3%

profile of v1, /device:TPU:1, one launch (start us, length us, event | category | flops | bytes accessed | tf_op | source)
XLA Modules:
  0.0 390.8 jit_solution(9991672749208934243)
XLA Ops:
  11.8 6.9 %all-to-all-start = ((bf16[8,2,512,128]{3,2,1,0:T(8,128)(2,1)}), bf16[8,2,512,128]{3,2,1,0:T(8,128)(2,1)S(1)}, u32[]{:S(2)}, u32[]{:S(2)}) async-start(bf16[8,2,512,128]{3,2,1,0:T(8,128)(2,1)} %paired.1), calls=%async_computation | async-start | bytes 4194304 | tf_op jit(solution)/shard_map/all_to_all | solution.py:42
  24.7 4.2 %collective-permute-done.1 = bf16[256,128]{0,1:T(8,128)(2,1)S(1)} collective-permute-done((bf16[256,128]{0,1:T(8,128)(2,1)S(1)}, bf16[256,128]{0,1:T(8,128)(2,1)S(1)}, u32[]{:S(2)}, u32[]{:S(2)}) %collective-permute-start.1) | collective-permute-done | bytes 65568 | tf_op jit(solution)/shard_map/ppermute | solution.py:334
  28.8 18.5 %all-to-all-done.both = bf16[8,2,512,128]{3,2,1,0:T(8,128)(2,1)S(1)} async-done(((bf16[8,2,512,128]{3,2,1,0:T(8,128)(2,1)}), bf16[8,2,512,128]{3,2,1,0:T(8,128)(2,1)S(1)}, u32[]{:S(2)}, u32[]{:S(2)}) %all-to-all-start) | async-done | bytes 2097184 | tf_op jit(solution)/shard_map/all_to_all | solution.py:42
  49.4 10.8 %all-to-all-start.1 = ((bf16[8,512,128]{2,1,0:T(8,128)(2,1)}), bf16[8,512,128]{2,1,0:T(8,128)(2,1)S(1)}, u32[]{:S(2)}, u32[]{:S(2)}) async-start(bf16[8,512,128]{2,1,0:T(8,128)(2,1)} %get-tuple-element.43), calls=%async_computation.1 | async-start | bytes 2097152 | tf_op jit(solution)/shard_map/all_to_all | solution.py:42
  60.3 5.6 %all-gather.4.cloned.1.call-done.table = bf16[8,256,256]{2,1,0:T(8,128)(2,1)} async-done(((bf16[1,256,256]{2,1,0:T(8,128)(2,1)}), bf16[8,256,256]{2,1,0:T(8,128)(2,1)}) %all-gather.4.cloned.1.call-update) | async-done | bytes 1048592 | tf_op jit(solution)/shard_map/all_gather | solution.py:340
  65.9 22.7 %all-to-all-done.1.frame = bf16[8,512,128]{2,1,0:T(8,128)(2,1)S(1)} async-done(((bf16[8,512,128]{2,1,0:T(8,128)(2,1)}), bf16[8,512,128]{2,1,0:T(8,128)(2,1)S(1)}, u32[]{:S(2)}, u32[]{:S(2)}) %all-to-all-start.1) | async-done | bytes 1048608 | tf_op jit(solution)/shard_map/all_to_all | solution.py:42
  93.4 23.4 %all_to_all.132 = bf16[32,128,128]{2,1,0:T(8,128)(2,1)S(1)} all-to-all(bf16[32,128,128]{2,1,0:T(8,128)(2,1)S(1)} %bitcast.58), channel_id=1, replica_groups=mesh['x'=4,'z'=8,'y'=4,'core'=2] {'x','y','core'}, dimensions={0} | all-to-all | bytes 2097152 | tf_op jit(solution)/shard_map/all_to_all | solution.py:42
  117.7 20.8 %all_to_all.133 = bf16[32,128,128]{2,1,0:T(8,128)(2,1)S(1)} all-to-all(bf16[32,128,128]{2,1,0:T(8,128)(2,1)S(1)} %bitcast.46), channel_id=1, replica_groups=mesh['x'=4,'z'=8,'y'=4,'core'=2] {'x','y','core'}, dimensions={0} | all-to-all | bytes 2097152 | tf_op jit(solution)/shard_map/all_to_all | solution.py:42
  142.1 20.7 %all_to_all.134 = bf16[32,128,128]{2,1,0:T(8,128)(2,1)S(1)} all-to-all(bf16[32,128,128]{2,1,0:T(8,128)(2,1)S(1)} %bitcast.57), channel_id=1, replica_groups=mesh['x'=4,'z'=8,'y'=4,'core'=2] {'x','y','core'}, dimensions={0} | all-to-all | bytes 2097152 | tf_op jit(solution)/shard_map/all_to_all | solution.py:42
  164.7 4.6 %all-to-all-start.5 = ((bf16[32,128,128]{2,1,0:T(8,128)(2,1)}), bf16[32,128,128]{2,1,0:T(8,128)(2,1)}, u32[]{:S(2)}, u32[]{:S(2)}) async-start(bf16[32,128,128]{2,1,0:T(8,128)(2,1)} %bitcast.19), calls=%async_computation.5 | async-start | bytes 2097152 | tf_op jit(solution)/shard_map/all_to_all | solution.py:42
  169.3 16.8 %all-to-all-done.5 = bf16[32,128,128]{2,1,0:T(8,128)(2,1)} async-done(((bf16[32,128,128]{2,1,0:T(8,128)(2,1)}), bf16[32,128,128]{2,1,0:T(8,128)(2,1)}, u32[]{:S(2)}, u32[]{:S(2)}) %all-to-all-start.5) | async-done | bytes 1048608 | tf_op jit(solution)/shard_map/all_to_all | solution.py:42
  188.5 4.8 %forward.5 = (bf16[32,2,128,128]{3,2,1,0:T(8,128)(2,1)S(1)}, f32[8,512,128]{2,1,0:T(8,128)S(1)}, bf16[8,512,128]{2,1,0:T(8,128)(2,1)S(1)}, bf16[8,512,256]{2,1,0:T(8,128)(2,1)S(1)}) custom-call(bf16[4096,128]{1,0:T(8,128)(2,1)} %bitcast.20.returned, f32[8,512,128]{2,1,0:T(8,128)S(1)} %copy-done.18, bf16[512,512]{1,0:T(8,128)(2,1)S(1)} %copy-done.4, ...), custom_call_target="tpu_custom_call" | custom-call | flops 1610612736 | bytes 9437184 | tf_op jit(solution)/shard_map/forward/pallas_call | solution.py:379
  193.4 31.9 %all_to_all.135 = bf16[32,2,128,128]{3,2,1,0:T(8,128)(2,1)S(1)} all-to-all(bf16[32,2,128,128]{3,2,1,0:T(8,128)(2,1)S(1)} %get-tuple-element.61), channel_id=1, replica_groups=mesh['x'=4,'z'=8,'y'=4,'core'=2] {'x','y','core'}, dimensions={0} | all-to-all | bytes 4194304 | tf_op jit(solution)/shard_map/all_to_all | solution.py:42
  225.2 3.8 filter_twice.1
  229.1 20.7 %all_to_all.136 = bf16[32,128,128]{2,1,0:T(8,128)(2,1)S(1)} all-to-all(bf16[32,128,128]{2,1,0:T(8,128)(2,1)S(1)} %bitcast.59), channel_id=1, replica_groups=mesh['x'=4,'z'=8,'y'=4,'core'=2] {'x','y','core'}, dimensions={0} | all-to-all | bytes 2097152 | tf_op jit(solution)/shard_map/all_to_all | solution.py:42
  249.8 4.6 %adjoint.3 = (bf16[4096,128]{1,0:T(8,128)(2,1)S(1)}, f32[8,512,128]{2,1,0:T(8,128)S(1)}, f32[128,256]{1,0:T(8,128)S(1)}, f32[128,256]{1,0:T(8,128)S(1)}) custom-call(bf16[4096,128]{1,0:T(8,128)(2,1)S(1)} %bitcast.50, f32[8,512,128]{2,1,0:T(8,128)S(1)} %get-tuple-element.63.base, bf16[8,512,128]{2,1,0:T(8,128)(2,1)S(1)} %dynamic-slice_bitcast_fusion.target.rest_0_, ...), custom_call_target="tpu_custom_call" | custom-call | flops 2147483648 | bytes 11534336 | tf_op jit(solution)/shard_map/adjoint/pallas_call | solution.py:426
  254.3 20.7 %all_to_all.137 = bf16[32,128,128]{2,1,0:T(8,128)(2,1)S(1)} all-to-all(bf16[32,128,128]{2,1,0:T(8,128)(2,1)S(1)} %bitcast.55), channel_id=1, replica_groups=mesh['x'=4,'z'=8,'y'=4,'core'=2] {'x','y','core'}, dimensions={0} | all-to-all | bytes 2097152 | tf_op jit(solution)/shard_map/all_to_all | solution.py:42
  275.9 20.8 %all_to_all.138 = bf16[32,128,128]{2,1,0:T(8,128)(2,1)S(1)} all-to-all(bf16[32,128,128]{2,1,0:T(8,128)(2,1)S(1)} %bitcast.49), channel_id=1, replica_groups=mesh['x'=4,'z'=8,'y'=4,'core'=2] {'x','y','core'}, dimensions={0} | all-to-all | bytes 2097152 | tf_op jit(solution)/shard_map/all_to_all | solution.py:42
  296.7 4.6 %adjoint.4 = (bf16[4096,128]{1,0:T(8,128)(2,1)S(1)}, f32[8,512,128]{2,1,0:T(8,128)S(1)}, f32[128,256]{1,0:T(8,128)S(1)}, f32[128,256]{1,0:T(8,128)S(1)}) custom-call(bf16[4096,128]{1,0:T(8,128)(2,1)S(1)} %bitcast.52, f32[8,512,128]{2,1,0:T(8,128)S(1)} %get-tuple-element.69.base, bf16[8,512,128]{2,1,0:T(8,128)(2,1)S(1)} %copy-done.14, ...), custom_call_target="tpu_custom_call" | custom-call | flops 2147483648 | bytes 11534336 | tf_op jit(solution)/shard_map/adjoint/pallas_call | solution.py:426
  301.3 20.7 %all_to_all.139 = bf16[32,128,128]{2,1,0:T(8,128)(2,1)S(1)} all-to-all(bf16[32,128,128]{2,1,0:T(8,128)(2,1)S(1)} %bitcast.53), channel_id=1, replica_groups=mesh['x'=4,'z'=8,'y'=4,'core'=2] {'x','y','core'}, dimensions={0} | all-to-all | bytes 2097152 | tf_op jit(solution)/shard_map/all_to_all | solution.py:42
  322.8 20.8 %all_to_all.140 = bf16[32,128,128]{2,1,0:T(8,128)(2,1)S(1)} all-to-all(bf16[32,128,128]{2,1,0:T(8,128)(2,1)S(1)} %bitcast.44), channel_id=1, replica_groups=mesh['x'=4,'z'=8,'y'=4,'core'=2] {'x','y','core'}, dimensions={0} | all-to-all | bytes 2097152 | tf_op jit(solution)/shard_map/all_to_all | solution.py:42
  346.3 12.7 %all_to_all.141 = f32[32,16,128]{2,1,0:T(8,128)S(1)} all-to-all(f32[32,16,128]{2,1,0:T(8,128)S(1)} %bitcast.66), channel_id=1, replica_groups=mesh['x'=4,'z'=8,'y'=4,'core'=2] {'x','y','core'}, dimensions={0} | all-to-all | bytes 524288 | tf_op jit(solution)/shard_map/all_to_all | solution.py:42
  359.1 10.2 %all_to_all.142 = f32[8,16,128]{2,1,0:T(8,128)S(1)} all-to-all(f32[8,16,128]{2,1,0:T(8,128)S(1)} %broadcast_in_dim.50), channel_id=1, replica_groups=mesh['x'=4,'z'=8,'y'=4,'core'=2] {'z'}, dimensions={0} | all-to-all | bytes 131072 | tf_op jit(solution)/shard_map/all_to_all | solution.py:42
  369.3 13.9 %all_to_all.143 = f32[32,16,128]{2,1,0:T(8,128)S(1)} all-to-all(f32[32,16,128]{2,1,0:T(8,128)S(1)} %bitcast.70), channel_id=1, replica_groups=mesh['x'=4,'z'=8,'y'=4,'core'=2] {'x','y','core'}, dimensions={0} | all-to-all | bytes 524288 | tf_op jit(solution)/shard_map/all_to_all | solution.py:42
  (87 shorter events, 31.3 us)
Async XLA Ops:
  11.8 35.6 %all-to-all-start = ((bf16[8,2,512,128]{3,2,1,0:T(8,128)(2,1)}), bf16[8,2,512,128]{3,2,1,0:T(8,128)(2,1)S(1)}, u32[]{:S(2)}, u32[]{:S(2)}) async-start(bf16[8,2,512,128]{3,2,1,0:T(8,128)(2,1)} %paired.1), calls=%async_computation | async-start | bytes 4194304 | tf_op jit(solution)/shard_map/all_to_all | solution.py:42
  18.7 47.2 %all-gather.4.cloned.1.call-start = ((), (), s32[]{:S(2)}) async-start(), calls=%async_computation.15 | async-start | bytes 1179648 | tf_op jit(solution)/shard_map/all_gather | solution.py:340
  18.8 5.9 %collective-permute-start = (bf16[128,256]{0,1:T(8,128)(2,1)S(1)}, bf16[128,256]{0,1:T(8,128)(2,1)S(1)}, u32[]{:S(2)}, u32[]{:S(2)}) collective-permute-start(bf16[128,256]{0,1:T(8,128)(2,1)S(1)} %bitcast.75), channel_id=1, source_target_pairs={{0,0},{1,8},{2,16},{3,24},{4,32},{5,40},{6,48},{7,56},{8,1},{9,9},... | collective-permute-start | bytes 196616 | tf_op jit(solution)/shard_map/ppermute | solution.py:333
  21.6 7.2 %collective-permute-start.1 = (bf16[256,128]{0,1:T(8,128)(2,1)S(1)}, bf16[256,128]{0,1:T(8,128)(2,1)S(1)}, u32[]{:S(2)}, u32[]{:S(2)}) collective-permute-start(bf16[256,128]{0,1:T(8,128)(2,1)S(1)} %bitcast.76), channel_id=1, source_target_pairs={{0,0},{1,8},{2,16},{3,24},{4,32},{5,40},{6,48},{7,56},{8,1},{9,9},... | collective-permute-start | bytes 196616 | tf_op jit(solution)/shard_map/ppermute | solution.py:334
  49.4 39.2 %copy-start.24 = (f32[2]{0:T(128)S(1)}, f32[2]{0:T(128)}, u32[]{:S(2)}) copy-start(f32[2]{0:T(128)} %constant.52) | copy-start | bytes 28
  49.4 39.1 %all-to-all-start.1 = ((bf16[8,512,128]{2,1,0:T(8,128)(2,1)}), bf16[8,512,128]{2,1,0:T(8,128)(2,1)S(1)}, u32[]{:S(2)}, u32[]{:S(2)}) async-start(bf16[8,512,128]{2,1,0:T(8,128)(2,1)} %get-tuple-element.43), calls=%async_computation.1 | async-start | bytes 2097152 | tf_op jit(solution)/shard_map/all_to_all | solution.py:42
  60.3 30.0 %copy-start.23 = (f32[256]{0:T(256)S(1)}, f32[256]{0:T(256)}, u32[]{:S(2)}) copy-start(f32[256]{0:T(256)} %param.16) | copy-start | bytes 3076
  60.3 30.3 %copy-start.3 = (bf16[512,512]{1,0:T(8,128)(2,1)S(1)}, bf16[512,512]{1,0:T(8,128)(2,1)}, u32[]{:S(2)}) copy-start(bf16[512,512]{1,0:T(8,128)(2,1)} %constant.53.turned.rest_5_.rest_4_) | copy-start | bytes 1572868
  60.3 125.9 %all-gather.6.cloned.1.call-start = ((), (), s32[]{:S(2)}) async-start(), calls=%async_computation.16 | async-start | bytes 9437184 | tf_op jit(solution)/shard_map/all_gather | solution.py:347
  93.4 24.3 %copy-start.15 = (bf16[8,512,256]{2,1,0:T(8,128)(2,1)}, bf16[8,512,256]{2,1,0:T(8,128)(2,1)S(1)}, u32[]{:S(2)}) copy-start(bf16[8,512,256]{2,1,0:T(8,128)(2,1)S(1)} %get-tuple-element.77.rest_1_) | copy-start | bytes 6291460
  93.4 24.3 %copy-start.19 = (bf16[8,512,128]{2,1,0:T(8,128)(2,1)}, bf16[8,512,128]{2,1,0:T(8,128)(2,1)S(1)}, u32[]{:S(2)}) copy-start(bf16[8,512,128]{2,1,0:T(8,128)(2,1)S(1)} %get-tuple-element.76.rest_0_) | copy-start | bytes 3145732
  93.4 23.4 %copy-start.2 = (bf16[8,256,256]{2,1,0:T(8,128)(2,1)S(1)}, bf16[8,256,256]{2,1,0:T(8,128)(2,1)}, u32[]{:S(2)}) copy-start(bf16[8,256,256]{2,1,0:T(8,128)(2,1)} %all-gather.4.cloned.1.call-done.table) | copy-start | bytes 3145732
  117.7 20.8 %copy-start.4 = (bf16[512,512]{1,0:T(8,128)(2,1)S(1)}, bf16[512,512]{1,0:T(8,128)(2,1)}, u32[]{:S(2)}) copy-start(bf16[512,512]{1,0:T(8,128)(2,1)} %constant.54.fourier.rest_3_.rest_2_) | copy-start | bytes 1572868
  117.7 20.8 %copy-start.6 = (bf16[128,256]{1,0:T(8,128)(2,1)S(1)}, bf16[128,256]{1,0:T(8,128)(2,1)}, u32[]{:S(2)}) copy-start(bf16[128,256]{1,0:T(8,128)(2,1)} %copy-done.5) | copy-start | bytes 196612
  117.7 20.8 %copy-start.9 = (bf16[256,128]{1,0:T(8,128)(2,1)S(1)}, bf16[256,128]{1,0:T(8,128)(2,1)}, u32[]{:S(2)}) copy-start(bf16[256,128]{1,0:T(8,128)(2,1)} %copy-done.8) | copy-start | bytes 196612
  142.1 22.6 %copy-start.11 = (bf16[8,512,256]{2,1,0:T(8,128)(2,1)}, bf16[8,512,256]{2,1,0:T(8,128)(2,1)S(1)}, u32[]{:S(2)}) copy-start(bf16[8,512,256]{2,1,0:T(8,128)(2,1)S(1)} %get-tuple-element.71.rest_1_) | copy-start | bytes 6291460
  142.1 22.6 %copy-start.13 = (bf16[8,512,128]{2,1,0:T(8,128)(2,1)}, bf16[8,512,128]{2,1,0:T(8,128)(2,1)S(1)}, u32[]{:S(2)}) copy-start(bf16[8,512,128]{2,1,0:T(8,128)(2,1)S(1)} %get-tuple-element.70.rest_0_) | copy-start | bytes 3145732
  142.1 22.6 %copy-start.17 = (f32[8,512,128]{2,1,0:T(8,128)}, f32[8,512,128]{2,1,0:T(8,128)S(1)}, u32[]{:S(2)}) copy-start(f32[8,512,128]{2,1,0:T(8,128)S(1)} %get-tuple-element.59.before) | copy-start | bytes 6291460
  164.7 21.4 %all-to-all-start.5 = ((bf16[32,128,128]{2,1,0:T(8,128)(2,1)}), bf16[32,128,128]{2,1,0:T(8,128)(2,1)}, u32[]{:S(2)}, u32[]{:S(2)}) async-start(bf16[32,128,128]{2,1,0:T(8,128)(2,1)} %bitcast.19), calls=%async_computation.5 | async-start | bytes 2097152 | tf_op jit(solution)/shard_map/all_to_all | solution.py:42
  275.0 21.7 %copy-start.14 = (bf16[8,512,128]{2,1,0:T(8,128)(2,1)S(1)}, bf16[8,512,128]{2,1,0:T(8,128)(2,1)}, u32[]{:S(2)}) copy-start(bf16[8,512,128]{2,1,0:T(8,128)(2,1)} %copy-done.13) | copy-start | bytes 3145732
  275.9 20.8 %copy-start.12 = (bf16[8,512,256]{2,1,0:T(8,128)(2,1)S(1)}, bf16[8,512,256]{2,1,0:T(8,128)(2,1)}, u32[]{:S(2)}) copy-start(bf16[8,512,256]{2,1,0:T(8,128)(2,1)} %copy-done.11) | copy-start | bytes 6291460
  321.9 21.7 %copy-start.20 = (bf16[8,512,128]{2,1,0:T(8,128)(2,1)S(1)}, bf16[8,512,128]{2,1,0:T(8,128)(2,1)}, u32[]{:S(2)}) copy-start(bf16[8,512,128]{2,1,0:T(8,128)(2,1)} %copy-done.19) | copy-start | bytes 3145732
  322.8 20.8 %copy-start.16 = (bf16[8,512,256]{2,1,0:T(8,128)(2,1)S(1)}, bf16[8,512,256]{2,1,0:T(8,128)(2,1)}, u32[]{:S(2)}) copy-start(bf16[8,512,256]{2,1,0:T(8,128)(2,1)} %copy-done.15) | copy-start | bytes 6291460
  343.6 40.3 %copy-start.1 = (bf16[8,256,256]{2,1,0:T(8,128)(2,1)S(1)}, bf16[8,256,256]{2,1,0:T(8,128)(2,1)}, u32[]{:S(2)}) copy-start(bf16[8,256,256]{2,1,0:T(8,128)(2,1)} %param.15) | copy-start | bytes 3145732
  (9 other events, 43.4 us)
Sparse Core Ops, SparseCore 0:
  24.6 41.2 all-gather.3
  88.7 90.7 all-gather.5

commit v2 on v1

--- a/solution.py
+++ b/solution.py
@@ -16,7 +16,7 @@
 PLANE = ("x", "y", "core")
 MEMBER = ("y", "core")
 
-PAIR = 2
+PAIR = 4
 SHARE = 8
 VMEM = 24 * 1024 * 1024
 MOST = 58 * 1024 * 1024

time: 392 us -> 387 us (0.987)
  Pallas kernels: 37.6 us -> 32.9 us
where the time goes in v2:
time: 387 us; the launch traced here: 386 us
  blocking collectives  237 us (61%)
  waiting for transfers between devices  67.8 us (18%)
  Pallas kernels  32.9 us (9%)
  starting transfers between devices  28 us (7%)
  between operations  14.5 us (4%)
  local copies, waits for them, and re-layouts  5.59 us (1%)
    all_to_all x12, blocking collectives, exchange(): return lax.all_to_all(values, axes, split_axis=0, concat_axis=0, tiled=True)  237 us
    all_to_all x3, waiting for transfers between devices, exchange(): return lax.all_to_all(values, axes, split_axis=0, concat_axis=0, tiled=True)  57.9 us
    all_to_all x3, starting transfers between devices, exchange(): return lax.all_to_all(values, axes, split_axis=0, concat_axis=0, tiled=True)  22.4 us
    pallas_call x3, Pallas kernels, adjoint_of(): pl.pallas_call(functools.partial(adjoint_kernel, rows, first_one, last),...  9.25 us
    pallas_call x3, Pallas kernels, forward(): pl.pallas_call(kernel, out_shape=[shaped((owners, 2, lines // owners, cha...  9.01 us
  transfers between devices with their start and end apart: 7, of which 6 were waited for; matrix products, arithmetic and copies ran while one was open for 1% of the time, Pallas kernels for 3%

profile of v2, /device:TPU:1, one launch (start us, length us, event | category | flops | bytes accessed | tf_op | source)
XLA Modules:
  0.0 386.1 jit_solution(7879568545122776849)
XLA Ops:
  11.8 6.9 %all-to-all-start = ((bf16[8,2,512,128]{3,2,1,0:T(8,128)(2,1)}), bf16[8,2,512,128]{3,2,1,0:T(8,128)(2,1)S(1)}, u32[]{:S(2)}, u32[]{:S(2)}) async-start(bf16[8,2,512,128]{3,2,1,0:T(8,128)(2,1)} %paired.1), calls=%async_computation | async-start | bytes 4194304 | tf_op jit(solution)/shard_map/all_to_all | solution.py:42
  24.7 4.2 %collective-permute-done.1 = bf16[256,128]{0,1:T(8,128)(2,1)S(1)} collective-permute-done((bf16[256,128]{0,1:T(8,128)(2,1)S(1)}, bf16[256,128]{0,1:T(8,128)(2,1)S(1)}, u32[]{:S(2)}, u32[]{:S(2)}) %collective-permute-start.1) | collective-permute-done | bytes 65568 | tf_op jit(solution)/shard_map/ppermute | solution.py:334
  28.8 18.5 %all-to-all-done.both = bf16[8,2,512,128]{3,2,1,0:T(8,128)(2,1)S(1)} async-done(((bf16[8,2,512,128]{3,2,1,0:T(8,128)(2,1)}), bf16[8,2,512,128]{3,2,1,0:T(8,128)(2,1)S(1)}, u32[]{:S(2)}, u32[]{:S(2)}) %all-to-all-start) | async-done | bytes 2097184 | tf_op jit(solution)/shard_map/all_to_all | solution.py:42
  49.4 10.8 %all-to-all-start.1 = ((bf16[8,512,128]{2,1,0:T(8,128)(2,1)}), bf16[8,512,128]{2,1,0:T(8,128)(2,1)S(1)}, u32[]{:S(2)}, u32[]{:S(2)}) async-start(bf16[8,512,128]{2,1,0:T(8,128)(2,1)} %get-tuple-element.43), calls=%async_computation.1 | async-start | bytes 2097152 | tf_op jit(solution)/shard_map/all_to_all | solution.py:42
  60.3 5.6 %all-gather.4.cloned.1.call-done.table = bf16[8,256,256]{2,1,0:T(8,128)(2,1)} async-done(((bf16[1,256,256]{2,1,0:T(8,128)(2,1)}), bf16[8,256,256]{2,1,0:T(8,128)(2,1)}) %all-gather.4.cloned.1.call-update) | async-done | bytes 1048592 | tf_op jit(solution)/shard_map/all_gather | solution.py:340
  65.9 22.7 %all-to-all-done.1.frame = bf16[8,512,128]{2,1,0:T(8,128)(2,1)S(1)} async-done(((bf16[8,512,128]{2,1,0:T(8,128)(2,1)}), bf16[8,512,128]{2,1,0:T(8,128)(2,1)S(1)}, u32[]{:S(2)}, u32[]{:S(2)}) %all-to-all-start.1) | async-done | bytes 1048608 | tf_op jit(solution)/shard_map/all_to_all | solution.py:42
  92.7 23.4 %all_to_all.132 = bf16[32,128,128]{2,1,0:T(8,128)(2,1)S(1)} all-to-all(bf16[32,128,128]{2,1,0:T(8,128)(2,1)S(1)} %bitcast.58), channel_id=1, replica_groups=mesh['x'=4,'z'=8,'y'=4,'core'=2] {'x','y','core'}, dimensions={0} | all-to-all | bytes 2097152 | tf_op jit(solution)/shard_map/all_to_all | solution.py:42
  117.1 20.8 %all_to_all.133 = bf16[32,128,128]{2,1,0:T(8,128)(2,1)S(1)} all-to-all(bf16[32,128,128]{2,1,0:T(8,128)(2,1)S(1)} %bitcast.46), channel_id=1, replica_groups=mesh['x'=4,'z'=8,'y'=4,'core'=2] {'x','y','core'}, dimensions={0} | all-to-all | bytes 2097152 | tf_op jit(solution)/shard_map/all_to_all | solution.py:42
  140.8 20.7 %all_to_all.134 = bf16[32,128,128]{2,1,0:T(8,128)(2,1)S(1)} all-to-all(bf16[32,128,128]{2,1,0:T(8,128)(2,1)S(1)} %bitcast.57), channel_id=1, replica_groups=mesh['x'=4,'z'=8,'y'=4,'core'=2] {'x','y','core'}, dimensions={0} | all-to-all | bytes 2097152 | tf_op jit(solution)/shard_map/all_to_all | solution.py:42
  163.3 4.6 %all-to-all-start.5 = ((bf16[32,128,128]{2,1,0:T(8,128)(2,1)}), bf16[32,128,128]{2,1,0:T(8,128)(2,1)}, u32[]{:S(2)}, u32[]{:S(2)}) async-start(bf16[32,128,128]{2,1,0:T(8,128)(2,1)} %bitcast.19), calls=%async_computation.5 | async-start | bytes 2097152 | tf_op jit(solution)/shard_map/all_to_all | solution.py:42
  168.0 16.8 %all-to-all-done.5 = bf16[32,128,128]{2,1,0:T(8,128)(2,1)} async-done(((bf16[32,128,128]{2,1,0:T(8,128)(2,1)}), bf16[32,128,128]{2,1,0:T(8,128)(2,1)}, u32[]{:S(2)}, u32[]{:S(2)}) %all-to-all-start.5) | async-done | bytes 1048608 | tf_op jit(solution)/shard_map/all_to_all | solution.py:42
  187.1 4.1 %forward.5 = (bf16[32,2,128,128]{3,2,1,0:T(8,128)(2,1)S(1)}, f32[8,512,128]{2,1,0:T(8,128)S(1)}, bf16[8,512,128]{2,1,0:T(8,128)(2,1)S(1)}, bf16[8,512,256]{2,1,0:T(8,128)(2,1)S(1)}) custom-call(bf16[4096,128]{1,0:T(8,128)(2,1)} %bitcast.20.returned, f32[8,512,128]{2,1,0:T(8,128)S(1)} %copy-done.18, bf16[512,512]{1,0:T(8,128)(2,1)S(1)} %copy-done.4, ...), custom_call_target="tpu_custom_call" | custom-call | flops 1610612736 | bytes 9437184 | tf_op jit(solution)/shard_map/forward/pallas_call | solution.py:379
  191.2 31.9 %all_to_all.135 = bf16[32,2,128,128]{3,2,1,0:T(8,128)(2,1)S(1)} all-to-all(bf16[32,2,128,128]{3,2,1,0:T(8,128)(2,1)S(1)} %get-tuple-element.61), channel_id=1, replica_groups=mesh['x'=4,'z'=8,'y'=4,'core'=2] {'x','y','core'}, dimensions={0} | all-to-all | bytes 4194304 | tf_op jit(solution)/shard_map/all_to_all | solution.py:42
  223.1 3.8 filter_twice.1
  227.0 20.7 %all_to_all.136 = bf16[32,128,128]{2,1,0:T(8,128)(2,1)S(1)} all-to-all(bf16[32,128,128]{2,1,0:T(8,128)(2,1)S(1)} %bitcast.59), channel_id=1, replica_groups=mesh['x'=4,'z'=8,'y'=4,'core'=2] {'x','y','core'}, dimensions={0} | all-to-all | bytes 2097152 | tf_op jit(solution)/shard_map/all_to_all | solution.py:42
  247.7 3.5 adjoint.3
  251.2 20.7 %all_to_all.137 = bf16[32,128,128]{2,1,0:T(8,128)(2,1)S(1)} all-to-all(bf16[32,128,128]{2,1,0:T(8,128)(2,1)S(1)} %bitcast.55), channel_id=1, replica_groups=mesh['x'=4,'z'=8,'y'=4,'core'=2] {'x','y','core'}, dimensions={0} | all-to-all | bytes 2097152 | tf_op jit(solution)/shard_map/all_to_all | solution.py:42
  272.7 20.8 %all_to_all.138 = bf16[32,128,128]{2,1,0:T(8,128)(2,1)S(1)} all-to-all(bf16[32,128,128]{2,1,0:T(8,128)(2,1)S(1)} %bitcast.49), channel_id=1, replica_groups=mesh['x'=4,'z'=8,'y'=4,'core'=2] {'x','y','core'}, dimensions={0} | all-to-all | bytes 2097152 | tf_op jit(solution)/shard_map/all_to_all | solution.py:42
  293.5 3.5 adjoint.4
  297.0 20.7 %all_to_all.139 = bf16[32,128,128]{2,1,0:T(8,128)(2,1)S(1)} all-to-all(bf16[32,128,128]{2,1,0:T(8,128)(2,1)S(1)} %bitcast.53), channel_id=1, replica_groups=mesh['x'=4,'z'=8,'y'=4,'core'=2] {'x','y','core'}, dimensions={0} | all-to-all | bytes 2097152 | tf_op jit(solution)/shard_map/all_to_all | solution.py:42
  318.6 20.8 %all_to_all.140 = bf16[32,128,128]{2,1,0:T(8,128)(2,1)S(1)} all-to-all(bf16[32,128,128]{2,1,0:T(8,128)(2,1)S(1)} %bitcast.44), channel_id=1, replica_groups=mesh['x'=4,'z'=8,'y'=4,'core'=2] {'x','y','core'}, dimensions={0} | all-to-all | bytes 2097152 | tf_op jit(solution)/shard_map/all_to_all | solution.py:42
  341.7 12.7 %all_to_all.141 = f32[32,16,128]{2,1,0:T(8,128)S(1)} all-to-all(f32[32,16,128]{2,1,0:T(8,128)S(1)} %bitcast.66), channel_id=1, replica_groups=mesh['x'=4,'z'=8,'y'=4,'core'=2] {'x','y','core'}, dimensions={0} | all-to-all | bytes 524288 | tf_op jit(solution)/shard_map/all_to_all | solution.py:42
  354.5 10.2 %all_to_all.142 = f32[8,16,128]{2,1,0:T(8,128)S(1)} all-to-all(f32[8,16,128]{2,1,0:T(8,128)S(1)} %broadcast_in_dim.50), channel_id=1, replica_groups=mesh['x'=4,'z'=8,'y'=4,'core'=2] {'z'}, dimensions={0} | all-to-all | bytes 131072 | tf_op jit(solution)/shard_map/all_to_all | solution.py:42
  364.6 13.9 %all_to_all.143 = f32[32,16,128]{2,1,0:T(8,128)S(1)} all-to-all(f32[32,16,128]{2,1,0:T(8,128)S(1)} %bitcast.70), channel_id=1, replica_groups=mesh['x'=4,'z'=8,'y'=4,'core'=2] {'x','y','core'}, dimensions={0} | all-to-all | bytes 524288 | tf_op jit(solution)/shard_map/all_to_all | solution.py:42
  (87 shorter events, 29.4 us)
Async XLA Ops:
  11.8 35.6 %all-to-all-start = ((bf16[8,2,512,128]{3,2,1,0:T(8,128)(2,1)}), bf16[8,2,512,128]{3,2,1,0:T(8,128)(2,1)S(1)}, u32[]{:S(2)}, u32[]{:S(2)}) async-start(bf16[8,2,512,128]{3,2,1,0:T(8,128)(2,1)} %paired.1), calls=%async_computation | async-start | bytes 4194304 | tf_op jit(solution)/shard_map/all_to_all | solution.py:42
  18.7 47.2 %all-gather.4.cloned.1.call-start = ((), (), s32[]{:S(2)}) async-start(), calls=%async_computation.15 | async-start | bytes 1179648 | tf_op jit(solution)/shard_map/all_gather | solution.py:340
  18.8 5.9 %collective-permute-start = (bf16[128,256]{0,1:T(8,128)(2,1)S(1)}, bf16[128,256]{0,1:T(8,128)(2,1)S(1)}, u32[]{:S(2)}, u32[]{:S(2)}) collective-permute-start(bf16[128,256]{0,1:T(8,128)(2,1)S(1)} %bitcast.75), channel_id=1, source_target_pairs={{0,0},{1,8},{2,16},{3,24},{4,32},{5,40},{6,48},{7,56},{8,1},{9,9},... | collective-permute-start | bytes 196616 | tf_op jit(solution)/shard_map/ppermute | solution.py:333
  21.6 7.2 %collective-permute-start.1 = (bf16[256,128]{0,1:T(8,128)(2,1)S(1)}, bf16[256,128]{0,1:T(8,128)(2,1)S(1)}, u32[]{:S(2)}, u32[]{:S(2)}) collective-permute-start(bf16[256,128]{0,1:T(8,128)(2,1)S(1)} %bitcast.76), channel_id=1, source_target_pairs={{0,0},{1,8},{2,16},{3,24},{4,32},{5,40},{6,48},{7,56},{8,1},{9,9},... | collective-permute-start | bytes 196616 | tf_op jit(solution)/shard_map/ppermute | solution.py:334
  49.4 39.2 %copy-start.24 = (f32[2]{0:T(128)S(1)}, f32[2]{0:T(128)}, u32[]{:S(2)}) copy-start(f32[2]{0:T(128)} %constant.52) | copy-start | bytes 28
  49.4 39.1 %all-to-all-start.1 = ((bf16[8,512,128]{2,1,0:T(8,128)(2,1)}), bf16[8,512,128]{2,1,0:T(8,128)(2,1)S(1)}, u32[]{:S(2)}, u32[]{:S(2)}) async-start(bf16[8,512,128]{2,1,0:T(8,128)(2,1)} %get-tuple-element.43), calls=%async_computation.1 | async-start | bytes 2097152 | tf_op jit(solution)/shard_map/all_to_all | solution.py:42
  60.3 30.0 %copy-start.23 = (f32[256]{0:T(256)S(1)}, f32[256]{0:T(256)}, u32[]{:S(2)}) copy-start(f32[256]{0:T(256)} %param.16) | copy-start | bytes 3076
  60.3 30.3 %copy-start.3 = (bf16[512,512]{1,0:T(8,128)(2,1)S(1)}, bf16[512,512]{1,0:T(8,128)(2,1)}, u32[]{:S(2)}) copy-start(bf16[512,512]{1,0:T(8,128)(2,1)} %constant.53.turned.rest_5_.rest_4_) | copy-start | bytes 1572868
  60.3 124.5 %all-gather.6.cloned.1.call-start = ((), (), s32[]{:S(2)}) async-start(), calls=%async_computation.16 | async-start | bytes 9437184 | tf_op jit(solution)/shard_map/all_gather | solution.py:347
  92.7 24.3 %copy-start.15 = (bf16[8,512,256]{2,1,0:T(8,128)(2,1)}, bf16[8,512,256]{2,1,0:T(8,128)(2,1)S(1)}, u32[]{:S(2)}) copy-start(bf16[8,512,256]{2,1,0:T(8,128)(2,1)S(1)} %get-tuple-element.77.rest_1_) | copy-start | bytes 6291460
  92.7 24.3 %copy-start.19 = (bf16[8,512,128]{2,1,0:T(8,128)(2,1)}, bf16[8,512,128]{2,1,0:T(8,128)(2,1)S(1)}, u32[]{:S(2)}) copy-start(bf16[8,512,128]{2,1,0:T(8,128)(2,1)S(1)} %get-tuple-element.76.rest_0_) | copy-start | bytes 3145732
  92.7 23.4 %copy-start.2 = (bf16[8,256,256]{2,1,0:T(8,128)(2,1)S(1)}, bf16[8,256,256]{2,1,0:T(8,128)(2,1)}, u32[]{:S(2)}) copy-start(bf16[8,256,256]{2,1,0:T(8,128)(2,1)} %all-gather.4.cloned.1.call-done.table) | copy-start | bytes 3145732
  117.1 20.8 %copy-start.4 = (bf16[512,512]{1,0:T(8,128)(2,1)S(1)}, bf16[512,512]{1,0:T(8,128)(2,1)}, u32[]{:S(2)}) copy-start(bf16[512,512]{1,0:T(8,128)(2,1)} %constant.54.fourier.rest_3_.rest_2_) | copy-start | bytes 1572868
  117.1 20.8 %copy-start.6 = (bf16[128,256]{1,0:T(8,128)(2,1)S(1)}, bf16[128,256]{1,0:T(8,128)(2,1)}, u32[]{:S(2)}) copy-start(bf16[128,256]{1,0:T(8,128)(2,1)} %copy-done.5) | copy-start | bytes 196612
  117.1 20.8 %copy-start.9 = (bf16[256,128]{1,0:T(8,128)(2,1)S(1)}, bf16[256,128]{1,0:T(8,128)(2,1)}, u32[]{:S(2)}) copy-start(bf16[256,128]{1,0:T(8,128)(2,1)} %copy-done.8) | copy-start | bytes 196612
  140.7 22.6 %copy-start.11 = (bf16[8,512,256]{2,1,0:T(8,128)(2,1)}, bf16[8,512,256]{2,1,0:T(8,128)(2,1)S(1)}, u32[]{:S(2)}) copy-start(bf16[8,512,256]{2,1,0:T(8,128)(2,1)S(1)} %get-tuple-element.71.rest_1_) | copy-start | bytes 6291460
  140.7 22.6 %copy-start.13 = (bf16[8,512,128]{2,1,0:T(8,128)(2,1)}, bf16[8,512,128]{2,1,0:T(8,128)(2,1)S(1)}, u32[]{:S(2)}) copy-start(bf16[8,512,128]{2,1,0:T(8,128)(2,1)S(1)} %get-tuple-element.70.rest_0_) | copy-start | bytes 3145732
  140.8 22.6 %copy-start.17 = (f32[8,512,128]{2,1,0:T(8,128)}, f32[8,512,128]{2,1,0:T(8,128)S(1)}, u32[]{:S(2)}) copy-start(f32[8,512,128]{2,1,0:T(8,128)S(1)} %get-tuple-element.59.before) | copy-start | bytes 6291460
  163.3 21.4 %all-to-all-start.5 = ((bf16[32,128,128]{2,1,0:T(8,128)(2,1)}), bf16[32,128,128]{2,1,0:T(8,128)(2,1)}, u32[]{:S(2)}, u32[]{:S(2)}) async-start(bf16[32,128,128]{2,1,0:T(8,128)(2,1)} %bitcast.19), calls=%async_computation.5 | async-start | bytes 2097152 | tf_op jit(solution)/shard_map/all_to_all | solution.py:42
  271.8 21.7 %copy-start.14 = (bf16[8,512,128]{2,1,0:T(8,128)(2,1)S(1)}, bf16[8,512,128]{2,1,0:T(8,128)(2,1)}, u32[]{:S(2)}) copy-start(bf16[8,512,128]{2,1,0:T(8,128)(2,1)} %copy-done.13) | copy-start | bytes 3145732
  272.7 20.8 %copy-start.12 = (bf16[8,512,256]{2,1,0:T(8,128)(2,1)S(1)}, bf16[8,512,256]{2,1,0:T(8,128)(2,1)}, u32[]{:S(2)}) copy-start(bf16[8,512,256]{2,1,0:T(8,128)(2,1)} %copy-done.11) | copy-start | bytes 6291460
  317.7 21.7 %copy-start.20 = (bf16[8,512,128]{2,1,0:T(8,128)(2,1)S(1)}, bf16[8,512,128]{2,1,0:T(8,128)(2,1)}, u32[]{:S(2)}) copy-start(bf16[8,512,128]{2,1,0:T(8,128)(2,1)} %copy-done.19) | copy-start | bytes 3145732
  318.6 20.8 %copy-start.16 = (bf16[8,512,256]{2,1,0:T(8,128)(2,1)S(1)}, bf16[8,512,256]{2,1,0:T(8,128)(2,1)}, u32[]{:S(2)}) copy-start(bf16[8,512,256]{2,1,0:T(8,128)(2,1)} %copy-done.15) | copy-start | bytes 6291460
  339.4 39.9 %copy-start.1 = (bf16[8,256,256]{2,1,0:T(8,128)(2,1)S(1)}, bf16[8,256,256]{2,1,0:T(8,128)(2,1)}, u32[]{:S(2)}) copy-start(bf16[8,256,256]{2,1,0:T(8,128)(2,1)} %param.15) | copy-start | bytes 3145732
  (9 other events, 42.1 us)
Sparse Core Ops, SparseCore 0:
  24.6 41.2 all-gather.3
  88.7 90.7 all-gather.5

commit v3 on v2

--- a/solution.py
+++ b/solution.py
@@ -16,7 +16,7 @@
 PLANE = ("x", "y", "core")
 MEMBER = ("y", "core")
 
-PAIR = 4
+PAIR = 8
 SHARE = 8
 VMEM = 24 * 1024 * 1024
 MOST = 58 * 1024 * 1024

time: 387 us -> 386 us (level)
  transfers between devices with their start and end apart: 7 -> 7, of which waited for: 6 -> 6; matrix products, arithmetic and copies ran while one was open for 1% -> 1% of each run, Pallas kernels for 3% -> 2%
where the time goes in v3:
time: 386 us; the launch traced here: 385 us
  blocking collectives  237 us (61%)
  waiting for transfers between devices  67.8 us (18%)
  Pallas kernels  32.2 us (8%)
  starting transfers between devices  28 us (7%)
  between operations  14.5 us (4%)
  local copies, waits for them, and re-layouts  5.59 us (1%)
    all_to_all x12, blocking collectives, exchange(): return lax.all_to_all(values, axes, split_axis=0, concat_axis=0, tiled=True)  237 us
    all_to_all x3, waiting for transfers between devices, exchange(): return lax.all_to_all(values, axes, split_axis=0, concat_axis=0, tiled=True)  57.9 us
    all_to_all x3, starting transfers between devices, exchange(): return lax.all_to_all(values, axes, split_axis=0, concat_axis=0, tiled=True)  22.4 us
    pallas_call x3, Pallas kernels, forward(): pl.pallas_call(kernel, out_shape=[shaped((owners, 2, lines // owners, cha...  8.76 us
    pallas_call x3, Pallas kernels, adjoint_of(): pl.pallas_call(functools.partial(adjoint_kernel, rows, first_one, last),...  8.73 us
  transfers between devices with their start and end apart: 7, of which 6 were waited for; matrix products, arithmetic and copies ran while one was open for 1% of the time, Pallas kernels for 2%

profile of v3, /device:TPU:1, one launch (start us, length us, event | category | flops | bytes accessed | tf_op | source)
XLA Modules:
  0.0 385.4 jit_solution(15862125153429341006)
XLA Ops:
  11.8 6.9 %all-to-all-start = ((bf16[8,2,512,128]{3,2,1,0:T(8,128)(2,1)}), bf16[8,2,512,128]{3,2,1,0:T(8,128)(2,1)S(1)}, u32[]{:S(2)}, u32[]{:S(2)}) async-start(bf16[8,2,512,128]{3,2,1,0:T(8,128)(2,1)} %paired.1), calls=%async_computation | async-start | bytes 4194304 | tf_op jit(solution)/shard_map/all_to_all | solution.py:42
  24.7 4.2 %collective-permute-done.1 = bf16[256,128]{0,1:T(8,128)(2,1)S(1)} collective-permute-done((bf16[256,128]{0,1:T(8,128)(2,1)S(1)}, bf16[256,128]{0,1:T(8,128)(2,1)S(1)}, u32[]{:S(2)}, u32[]{:S(2)}) %collective-permute-start.1) | collective-permute-done | bytes 65568 | tf_op jit(solution)/shard_map/ppermute | solution.py:334
  28.8 18.5 %all-to-all-done.both = bf16[8,2,512,128]{3,2,1,0:T(8,128)(2,1)S(1)} async-done(((bf16[8,2,512,128]{3,2,1,0:T(8,128)(2,1)}), bf16[8,2,512,128]{3,2,1,0:T(8,128)(2,1)S(1)}, u32[]{:S(2)}, u32[]{:S(2)}) %all-to-all-start) | async-done | bytes 2097184 | tf_op jit(solution)/shard_map/all_to_all | solution.py:42
  49.4 10.8 %all-to-all-start.1 = ((bf16[8,512,128]{2,1,0:T(8,128)(2,1)}), bf16[8,512,128]{2,1,0:T(8,128)(2,1)S(1)}, u32[]{:S(2)}, u32[]{:S(2)}) async-start(bf16[8,512,128]{2,1,0:T(8,128)(2,1)} %get-tuple-element.43), calls=%async_computation.1 | async-start | bytes 2097152 | tf_op jit(solution)/shard_map/all_to_all | solution.py:42
  60.3 5.6 %all-gather.4.cloned.1.call-done.table = bf16[8,256,256]{2,1,0:T(8,128)(2,1)} async-done(((bf16[1,256,256]{2,1,0:T(8,128)(2,1)}), bf16[8,256,256]{2,1,0:T(8,128)(2,1)}) %all-gather.4.cloned.1.call-update) | async-done | bytes 1048592 | tf_op jit(solution)/shard_map/all_gather | solution.py:340
  65.9 22.7 %all-to-all-done.1.frame = bf16[8,512,128]{2,1,0:T(8,128)(2,1)S(1)} async-done(((bf16[8,512,128]{2,1,0:T(8,128)(2,1)}), bf16[8,512,128]{2,1,0:T(8,128)(2,1)S(1)}, u32[]{:S(2)}, u32[]{:S(2)}) %all-to-all-start.1) | async-done | bytes 1048608 | tf_op jit(solution)/shard_map/all_to_all | solution.py:42
  92.6 23.4 %all_to_all.132 = bf16[32,128,128]{2,1,0:T(8,128)(2,1)S(1)} all-to-all(bf16[32,128,128]{2,1,0:T(8,128)(2,1)S(1)} %bitcast.58), channel_id=1, replica_groups=mesh['x'=4,'z'=8,'y'=4,'core'=2] {'x','y','core'}, dimensions={0} | all-to-all | bytes 2097152 | tf_op jit(solution)/shard_map/all_to_all | solution.py:42
  117.0 20.8 %all_to_all.133 = bf16[32,128,128]{2,1,0:T(8,128)(2,1)S(1)} all-to-all(bf16[32,128,128]{2,1,0:T(8,128)(2,1)S(1)} %bitcast.46), channel_id=1, replica_groups=mesh['x'=4,'z'=8,'y'=4,'core'=2] {'x','y','core'}, dimensions={0} | all-to-all | bytes 2097152 | tf_op jit(solution)/shard_map/all_to_all | solution.py:42
  140.6 20.7 %all_to_all.134 = bf16[32,128,128]{2,1,0:T(8,128)(2,1)S(1)} all-to-all(bf16[32,128,128]{2,1,0:T(8,128)(2,1)S(1)} %bitcast.57), channel_id=1, replica_groups=mesh['x'=4,'z'=8,'y'=4,'core'=2] {'x','y','core'}, dimensions={0} | all-to-all | bytes 2097152 | tf_op jit(solution)/shard_map/all_to_all | solution.py:42
  163.1 4.6 %all-to-all-start.5 = ((bf16[32,128,128]{2,1,0:T(8,128)(2,1)}), bf16[32,128,128]{2,1,0:T(8,128)(2,1)}, u32[]{:S(2)}, u32[]{:S(2)}) async-start(bf16[32,128,128]{2,1,0:T(8,128)(2,1)} %bitcast.19), calls=%async_computation.5 | async-start | bytes 2097152 | tf_op jit(solution)/shard_map/all_to_all | solution.py:42
  167.8 16.8 %all-to-all-done.5 = bf16[32,128,128]{2,1,0:T(8,128)(2,1)} async-done(((bf16[32,128,128]{2,1,0:T(8,128)(2,1)}), bf16[32,128,128]{2,1,0:T(8,128)(2,1)}, u32[]{:S(2)}, u32[]{:S(2)}) %all-to-all-start.5) | async-done | bytes 1048608 | tf_op jit(solution)/shard_map/all_to_all | solution.py:42
  186.9 4.0 %forward.5 = (bf16[32,2,128,128]{3,2,1,0:T(8,128)(2,1)S(1)}, f32[8,512,128]{2,1,0:T(8,128)S(1)}, bf16[8,512,128]{2,1,0:T(8,128)(2,1)S(1)}, bf16[8,512,256]{2,1,0:T(8,128)(2,1)S(1)}) custom-call(bf16[4096,128]{1,0:T(8,128)(2,1)} %bitcast.20.returned, f32[8,512,128]{2,1,0:T(8,128)S(1)} %copy-done.18, bf16[512,512]{1,0:T(8,128)(2,1)S(1)} %copy-done.4, ...), custom_call_target="tpu_custom_call" | custom-call | flops 1610612736 | bytes 9437184 | tf_op jit(solution)/shard_map/forward/pallas_call | solution.py:379
  191.0 31.9 %all_to_all.135 = bf16[32,2,128,128]{3,2,1,0:T(8,128)(2,1)S(1)} all-to-all(bf16[32,2,128,128]{3,2,1,0:T(8,128)(2,1)S(1)} %get-tuple-element.61), channel_id=1, replica_groups=mesh['x'=4,'z'=8,'y'=4,'core'=2] {'x','y','core'}, dimensions={0} | all-to-all | bytes 4194304 | tf_op jit(solution)/shard_map/all_to_all | solution.py:42
  222.9 3.8 filter_twice.1
  226.7 20.7 %all_to_all.136 = bf16[32,128,128]{2,1,0:T(8,128)(2,1)S(1)} all-to-all(bf16[32,128,128]{2,1,0:T(8,128)(2,1)S(1)} %bitcast.59), channel_id=1, replica_groups=mesh['x'=4,'z'=8,'y'=4,'core'=2] {'x','y','core'}, dimensions={0} | all-to-all | bytes 2097152 | tf_op jit(solution)/shard_map/all_to_all | solution.py:42
  247.4 3.3 adjoint.3
  250.7 20.7 %all_to_all.137 = bf16[32,128,128]{2,1,0:T(8,128)(2,1)S(1)} all-to-all(bf16[32,128,128]{2,1,0:T(8,128)(2,1)S(1)} %bitcast.55), channel_id=1, replica_groups=mesh['x'=4,'z'=8,'y'=4,'core'=2] {'x','y','core'}, dimensions={0} | all-to-all | bytes 2097152 | tf_op jit(solution)/shard_map/all_to_all | solution.py:42
  272.3 20.8 %all_to_all.138 = bf16[32,128,128]{2,1,0:T(8,128)(2,1)S(1)} all-to-all(bf16[32,128,128]{2,1,0:T(8,128)(2,1)S(1)} %bitcast.49), channel_id=1, replica_groups=mesh['x'=4,'z'=8,'y'=4,'core'=2] {'x','y','core'}, dimensions={0} | all-to-all | bytes 2097152 | tf_op jit(solution)/shard_map/all_to_all | solution.py:42
  293.1 3.3 adjoint.4
  296.4 20.7 %all_to_all.139 = bf16[32,128,128]{2,1,0:T(8,128)(2,1)S(1)} all-to-all(bf16[32,128,128]{2,1,0:T(8,128)(2,1)S(1)} %bitcast.53), channel_id=1, replica_groups=mesh['x'=4,'z'=8,'y'=4,'core'=2] {'x','y','core'}, dimensions={0} | all-to-all | bytes 2097152 | tf_op jit(solution)/shard_map/all_to_all | solution.py:42
  317.9 20.8 %all_to_all.140 = bf16[32,128,128]{2,1,0:T(8,128)(2,1)S(1)} all-to-all(bf16[32,128,128]{2,1,0:T(8,128)(2,1)S(1)} %bitcast.44), channel_id=1, replica_groups=mesh['x'=4,'z'=8,'y'=4,'core'=2] {'x','y','core'}, dimensions={0} | all-to-all | bytes 2097152 | tf_op jit(solution)/shard_map/all_to_all | solution.py:42
  340.9 12.7 %all_to_all.141 = f32[32,16,128]{2,1,0:T(8,128)S(1)} all-to-all(f32[32,16,128]{2,1,0:T(8,128)S(1)} %bitcast.66), channel_id=1, replica_groups=mesh['x'=4,'z'=8,'y'=4,'core'=2] {'x','y','core'}, dimensions={0} | all-to-all | bytes 524288 | tf_op jit(solution)/shard_map/all_to_all | solution.py:42
  353.7 10.2 %all_to_all.142 = f32[8,16,128]{2,1,0:T(8,128)S(1)} all-to-all(f32[8,16,128]{2,1,0:T(8,128)S(1)} %broadcast_in_dim.50), channel_id=1, replica_groups=mesh['x'=4,'z'=8,'y'=4,'core'=2] {'z'}, dimensions={0} | all-to-all | bytes 131072 | tf_op jit(solution)/shard_map/all_to_all | solution.py:42
  363.9 13.9 %all_to_all.143 = f32[32,16,128]{2,1,0:T(8,128)S(1)} all-to-all(f32[32,16,128]{2,1,0:T(8,128)S(1)} %bitcast.70), channel_id=1, replica_groups=mesh['x'=4,'z'=8,'y'=4,'core'=2] {'x','y','core'}, dimensions={0} | all-to-all | bytes 524288 | tf_op jit(solution)/shard_map/all_to_all | solution.py:42
  (87 shorter events, 29.1 us)
Async XLA Ops:
  11.8 35.6 %all-to-all-start = ((bf16[8,2,512,128]{3,2,1,0:T(8,128)(2,1)}), bf16[8,2,512,128]{3,2,1,0:T(8,128)(2,1)S(1)}, u32[]{:S(2)}, u32[]{:S(2)}) async-start(bf16[8,2,512,128]{3,2,1,0:T(8,128)(2,1)} %paired.1), calls=%async_computation | async-start | bytes 4194304 | tf_op jit(solution)/shard_map/all_to_all | solution.py:42
  18.7 47.2 %all-gather.4.cloned.1.call-start = ((), (), s32[]{:S(2)}) async-start(), calls=%async_computation.15 | async-start | bytes 1179648 | tf_op jit(solution)/shard_map/all_gather | solution.py:340
  18.8 5.9 %collective-permute-start = (bf16[128,256]{0,1:T(8,128)(2,1)S(1)}, bf16[128,256]{0,1:T(8,128)(2,1)S(1)}, u32[]{:S(2)}, u32[]{:S(2)}) collective-permute-start(bf16[128,256]{0,1:T(8,128)(2,1)S(1)} %bitcast.75), channel_id=1, source_target_pairs={{0,0},{1,8},{2,16},{3,24},{4,32},{5,40},{6,48},{7,56},{8,1},{9,9},... | collective-permute-start | bytes 196616 | tf_op jit(solution)/shard_map/ppermute | solution.py:333
  21.6 7.2 %collective-permute-start.1 = (bf16[256,128]{0,1:T(8,128)(2,1)S(1)}, bf16[256,128]{0,1:T(8,128)(2,1)S(1)}, u32[]{:S(2)}, u32[]{:S(2)}) collective-permute-start(bf16[256,128]{0,1:T(8,128)(2,1)S(1)} %bitcast.76), channel_id=1, source_target_pairs={{0,0},{1,8},{2,16},{3,24},{4,32},{5,40},{6,48},{7,56},{8,1},{9,9},... | collective-permute-start | bytes 196616 | tf_op jit(solution)/shard_map/ppermute | solution.py:334
  49.4 39.2 %copy-start.24 = (f32[2]{0:T(128)S(1)}, f32[2]{0:T(128)}, u32[]{:S(2)}) copy-start(f32[2]{0:T(128)} %constant.52) | copy-start | bytes 28
  49.4 39.1 %all-to-all-start.1 = ((bf16[8,512,128]{2,1,0:T(8,128)(2,1)}), bf16[8,512,128]{2,1,0:T(8,128)(2,1)S(1)}, u32[]{:S(2)}, u32[]{:S(2)}) async-start(bf16[8,512,128]{2,1,0:T(8,128)(2,1)} %get-tuple-element.43), calls=%async_computation.1 | async-start | bytes 2097152 | tf_op jit(solution)/shard_map/all_to_all | solution.py:42
  60.3 30.0 %copy-start.23 = (f32[256]{0:T(256)S(1)}, f32[256]{0:T(256)}, u32[]{:S(2)}) copy-start(f32[256]{0:T(256)} %param.16) | copy-start | bytes 3076
  60.3 30.3 %copy-start.3 = (bf16[512,512]{1,0:T(8,128)(2,1)S(1)}, bf16[512,512]{1,0:T(8,128)(2,1)}, u32[]{:S(2)}) copy-start(bf16[512,512]{1,0:T(8,128)(2,1)} %constant.53.turned.rest_5_.rest_4_) | copy-start | bytes 1572868
  60.3 124.3 %all-gather.6.cloned.1.call-start = ((), (), s32[]{:S(2)}) async-start(), calls=%async_computation.16 | async-start | bytes 9437184 | tf_op jit(solution)/shard_map/all_gather | solution.py:347
  92.6 24.3 %copy-start.15 = (bf16[8,512,256]{2,1,0:T(8,128)(2,1)}, bf16[8,512,256]{2,1,0:T(8,128)(2,1)S(1)}, u32[]{:S(2)}) copy-start(bf16[8,512,256]{2,1,0:T(8,128)(2,1)S(1)} %get-tuple-element.77.rest_1_) | copy-start | bytes 6291460
  92.6 24.3 %copy-start.19 = (bf16[8,512,128]{2,1,0:T(8,128)(2,1)}, bf16[8,512,128]{2,1,0:T(8,128)(2,1)S(1)}, u32[]{:S(2)}) copy-start(bf16[8,512,128]{2,1,0:T(8,128)(2,1)S(1)} %get-tuple-element.76.rest_0_) | copy-start | bytes 3145732
  92.6 23.4 %copy-start.2 = (bf16[8,256,256]{2,1,0:T(8,128)(2,1)S(1)}, bf16[8,256,256]{2,1,0:T(8,128)(2,1)}, u32[]{:S(2)}) copy-start(bf16[8,256,256]{2,1,0:T(8,128)(2,1)} %all-gather.4.cloned.1.call-done.table) | copy-start | bytes 3145732
  117.0 20.8 %copy-start.4 = (bf16[512,512]{1,0:T(8,128)(2,1)S(1)}, bf16[512,512]{1,0:T(8,128)(2,1)}, u32[]{:S(2)}) copy-start(bf16[512,512]{1,0:T(8,128)(2,1)} %constant.54.fourier.rest_3_.rest_2_) | copy-start | bytes 1572868
  117.0 20.8 %copy-start.6 = (bf16[128,256]{1,0:T(8,128)(2,1)S(1)}, bf16[128,256]{1,0:T(8,128)(2,1)}, u32[]{:S(2)}) copy-start(bf16[128,256]{1,0:T(8,128)(2,1)} %copy-done.5) | copy-start | bytes 196612
  117.0 20.8 %copy-start.9 = (bf16[256,128]{1,0:T(8,128)(2,1)S(1)}, bf16[256,128]{1,0:T(8,128)(2,1)}, u32[]{:S(2)}) copy-start(bf16[256,128]{1,0:T(8,128)(2,1)} %copy-done.8) | copy-start | bytes 196612
  140.5 22.6 %copy-start.11 = (bf16[8,512,256]{2,1,0:T(8,128)(2,1)}, bf16[8,512,256]{2,1,0:T(8,128)(2,1)S(1)}, u32[]{:S(2)}) copy-start(bf16[8,512,256]{2,1,0:T(8,128)(2,1)S(1)} %get-tuple-element.71.rest_1_) | copy-start | bytes 6291460
  140.6 22.6 %copy-start.13 = (bf16[8,512,128]{2,1,0:T(8,128)(2,1)}, bf16[8,512,128]{2,1,0:T(8,128)(2,1)S(1)}, u32[]{:S(2)}) copy-start(bf16[8,512,128]{2,1,0:T(8,128)(2,1)S(1)} %get-tuple-element.70.rest_0_) | copy-start | bytes 3145732
  140.6 22.6 %copy-start.17 = (f32[8,512,128]{2,1,0:T(8,128)}, f32[8,512,128]{2,1,0:T(8,128)S(1)}, u32[]{:S(2)}) copy-start(f32[8,512,128]{2,1,0:T(8,128)S(1)} %get-tuple-element.59.before) | copy-start | bytes 6291460
  163.1 21.4 %all-to-all-start.5 = ((bf16[32,128,128]{2,1,0:T(8,128)(2,1)}), bf16[32,128,128]{2,1,0:T(8,128)(2,1)}, u32[]{:S(2)}, u32[]{:S(2)}) async-start(bf16[32,128,128]{2,1,0:T(8,128)(2,1)} %bitcast.19), calls=%async_computation.5 | async-start | bytes 2097152 | tf_op jit(solution)/shard_map/all_to_all | solution.py:42
  271.4 21.7 %copy-start.14 = (bf16[8,512,128]{2,1,0:T(8,128)(2,1)S(1)}, bf16[8,512,128]{2,1,0:T(8,128)(2,1)}, u32[]{:S(2)}) copy-start(bf16[8,512,128]{2,1,0:T(8,128)(2,1)} %copy-done.13) | copy-start | bytes 3145732
  272.3 20.8 %copy-start.12 = (bf16[8,512,256]{2,1,0:T(8,128)(2,1)S(1)}, bf16[8,512,256]{2,1,0:T(8,128)(2,1)}, u32[]{:S(2)}) copy-start(bf16[8,512,256]{2,1,0:T(8,128)(2,1)} %copy-done.11) | copy-start | bytes 6291460
  317.1 21.7 %copy-start.20 = (bf16[8,512,128]{2,1,0:T(8,128)(2,1)S(1)}, bf16[8,512,128]{2,1,0:T(8,128)(2,1)}, u32[]{:S(2)}) copy-start(bf16[8,512,128]{2,1,0:T(8,128)(2,1)} %copy-done.19) | copy-start | bytes 3145732
  317.9 20.8 %copy-start.16 = (bf16[8,512,256]{2,1,0:T(8,128)(2,1)S(1)}, bf16[8,512,256]{2,1,0:T(8,128)(2,1)}, u32[]{:S(2)}) copy-start(bf16[8,512,256]{2,1,0:T(8,128)(2,1)} %copy-done.15) | copy-start | bytes 6291460
  338.8 39.8 %copy-start.1 = (bf16[8,256,256]{2,1,0:T(8,128)(2,1)S(1)}, bf16[8,256,256]{2,1,0:T(8,128)(2,1)}, u32[]{:S(2)}) copy-start(bf16[8,256,256]{2,1,0:T(8,128)(2,1)} %param.15) | copy-start | bytes 3145732
  (9 other events, 41.9 us)
Sparse Core Ops, SparseCore 0:
  24.6 41.2 all-gather.3
  88.7 90.7 all-gather.5
